TPU v7x, 256 devices: a whole 4x4x8 slice. The times are simulated.
256 devices in a mesh: grp: 8 (over x, y_lo), dp: 32 (over y_hi, z, core).
Axes of the slice: x: 4, y: 4 (y_hi: 2, y_lo: 2; y = y_hi * 2 + y_lo), z: 8, core: 2. Of those that a mesh axis runs over, the one named last changes fastest.
Arguments:
- latents: bfloat16 [256, 16, 128, 320], P(('grp', 'dp')), may hold values from -6 to 6
- cotangent: bfloat16 [256, 16, 128, 320], P(('grp', 'dp')), may hold values from -6 to 6
- weight: bfloat16 [3, 3, 320, 320], replicated, may hold values from -0.109375 to 0.109375
- gain: float32 [320], replicated, may hold values from 0.25 to 1.75
- shift: float32 [320], replicated, may hold values from -3 to 3
- master: float32 [950272], P(('grp', 'dp')), may hold values from -0.109375 to 0.109375
- first_moment: float32 [950272], P(('grp', 'dp')), may hold values from -0.0014648438 to 0.0014648438
- second_moment: float32 [950272], P(('grp', 'dp')), may hold values from 1e-08 to 1e-06
Outputs:
- grad_input: bfloat16 [256, 16, 128, 320], P(('grp', 'dp'))
- new_weight: bfloat16 [3, 3, 320, 320], replicated
- new_bias: bfloat16 [320], replicated
- new_gain: bfloat16 [320], replicated
- new_shift: bfloat16 [320], replicated
- new_master: float32 [950272], P(('grp', 'dp'))
- new_first: float32 [950272], P(('grp', 'dp'))
- new_second: float32 [950272], P(('grp', 'dp'))
All inputs are finite; a program needn't handle non-finite values.
Results may differ from a plain program's by a relative error of at most 0.0033.
Values may be sent and summed in bfloat16 or wider, within the bound.
A program may use at most 64 MiB of HBM per device.

v0:
```python
import jax
import jax.numpy as jnp
from jax import lax
from jax.sharding import PartitionSpec as P

GROUPS = 32


norm_epsilon = 1e-05
beta_first = 0.9
beta_second = 0.999
adam_epsilon = 1e-08
learn_rate = 0.001
weight_decay = 0.01
clip_limit = 1.0
correct_first = 1.0
correct_second = 0.6323045752290363


def norm_act(entries, gain, shift):
    height, breadth, channels = entries.shape
    grouped = entries.reshape(height * breadth, GROUPS, channels // GROUPS)
    centre = jnp.mean(grouped, axis=(0, 2), keepdims=True)
    centred = grouped - centre
    spread = jnp.mean(centred * centred, axis=(0, 2), keepdims=True)
    normed = (centred * lax.rsqrt(spread + norm_epsilon)).reshape(height, breadth, channels)
    return jax.nn.silu(normed * gain + shift)


def local_grads(sample, cot_sample, weight, gain, shift):
    height, breadth, channels = sample.shape
    activation, pullback = jax.vjp(norm_act, sample.astype(jnp.float32), gain, shift)
    stored = activation.astype(jnp.bfloat16)
    padded = jnp.pad(stored, ((1, 1), (1, 1), (0, 0)))
    cot_rows = cot_sample.reshape(height * breadth, channels)
    padded_grad = jnp.zeros((height + 2, breadth + 2, channels), jnp.float32)
    kernels = []
    for tap_row in range(3):
        for tap_col in range(3):
            window = padded[tap_row : tap_row + height, tap_col : tap_col + breadth].reshape(
                height * breadth, channels
            )
            kernels.append(
                lax.dot_general(
                    window, cot_rows, (((0,), (0,)), ((), ())), preferred_element_type=jnp.float32
                )
            )
            back = lax.dot_general(
                cot_rows,
                weight[tap_row, tap_col],
                (((1,), (1,)), ((), ())),
                preferred_element_type=jnp.float32,
            )
            padded_grad = padded_grad.at[
                tap_row : tap_row + height, tap_col : tap_col + breadth
            ].add(back.reshape(height, breadth, channels))
    grad_act = padded_grad[1:-1, 1:-1]
    grad_in, grad_gain, grad_shift = pullback(grad_act)
    grad_bias = jnp.sum(cot_rows.astype(jnp.float32), axis=0)
    kernel_grad = jnp.stack(kernels).reshape(-1)
    flat_grad = jnp.concatenate([kernel_grad, grad_bias, grad_gain, grad_shift])
    return (grad_in.astype(jnp.bfloat16), flat_grad)


def on_device(latents, cotangent, weight, gain, shift, master, first_moment, second_moment):
    groups_count = lax.axis_size("grp")
    owners_count = lax.axis_size("dp")
    shard_len = master.shape[0]
    flat_len = shard_len * groups_count * owners_count
    grad_in, flat_grad = local_grads(latents[0], cotangent[0], weight, gain, shift)
    padded_flat = jnp.concatenate(
        [flat_grad, jnp.zeros((flat_len - flat_grad.shape[0],), jnp.float32)]
    )
    grouped = padded_flat.reshape(groups_count, owners_count * shard_len)
    within = lax.psum_scatter(grouped, "dp", scatter_dimension=1, tiled=True)
    summed = lax.psum_scatter(within, "grp", scatter_dimension=0, tiled=True).reshape(shard_len)
    norm_total = lax.psum(jnp.sum(summed * summed), ("grp", "dp"))
    clip = jnp.minimum(1.0, clip_limit / (jnp.sqrt(norm_total) + 1e-06))
    clipped = clip * summed
    new_first = beta_first * first_moment + (1.0 - beta_first) * clipped
    new_second = beta_second * second_moment + (1.0 - beta_second) * clipped * clipped
    step_dir = new_first / correct_first / (jnp.sqrt(new_second / correct_second) + adam_epsilon)
    new_master = master - learn_rate * (step_dir + weight_decay * master)
    rounded = new_master.astype(jnp.bfloat16)
    whole = lax.all_gather(rounded, ("grp", "dp"), axis=0, tiled=True)
    channels = weight.shape[2]
    kernel_size = 9 * channels * channels
    new_weight = whole[:kernel_size].reshape(3, 3, channels, channels)
    new_bias = whole[kernel_size : kernel_size + channels]
    new_gain = whole[kernel_size + channels : kernel_size + 2 * channels]
    new_shift = whole[kernel_size + 2 * channels : kernel_size + 3 * channels]
    return (
        grad_in[None],
        new_weight,
        new_bias,
        new_gain,
        new_shift,
        new_master,
        new_first,
        new_second,
    )


def solution(mesh):
    in_specs = (
        P(("grp", "dp"), None, None, None),
        P(("grp", "dp"), None, None, None),
        P(),
        P(),
        P(),
        P(("grp", "dp")),
        P(("grp", "dp")),
        P(("grp", "dp")),
    )
    out_specs = (
        P(("grp", "dp"), None, None, None),
        P(),
        P(),
        P(),
        P(),
        P(("grp", "dp")),
        P(("grp", "dp")),
        P(("grp", "dp")),
    )
    return jax.shard_map(
        on_device, mesh=mesh, in_specs=in_specs, out_specs=out_specs, check_vma=False
    )
```

profile of v0, /device:TPU:1, one launch (start us, length us, event | category | flops | bytes accessed | tf_op | source)
XLA Modules:
  0.0 940.0 jit_solution(12574686273717778876)
XLA Ops:
  18.6 4.6 dynamic-slice_add_fusion
  24.0 15.5 %scatter-add.31 = f32[18,130,320]{1,2,0:T(8,128)} dynamic-update-slice(f32[18,130,320]{1,2,0:T(8,128)} %scatter-add.30, f32[16,128,320]{1,2,0:T(8,128)} %dynamic-slice_add_fusion, s32[]{:T(128)} %bitcast.3, s32[]{:T(128)} %bitcast.4, s32[]{:T(128)} %constant.286.clone.1) | dynamic-update-slice | bytes 5242884 | tf_op jit(solution)/shard_map/scatter-add | solution.py:56
  39.5 6.9 add_select_fusion
  46.4 15.3 %scatter-add.34 = f32[18,130,320]{1,2,0:T(8,128)} dynamic-update-slice(f32[18,130,320]{1,2,0:T(8,128)} %scatter-add.31, f32[16,128,320]{1,2,0:T(8,128)} %add_select_fusion, s32[]{:T(128)} %bitcast.7, s32[]{:T(128)} %bitcast.8, s32[]{:T(128)} %constant.286.clone.1) | dynamic-update-slice | bytes 5242884 | tf_op jit(solution)/shard_map/scatter-add | solution.py:56
  61.8 4.3 fusion.30
  66.1 5.0 slice_add_fusion.4
  71.1 14.0 %scatter-add.36 = f32[18,130,320]{1,2,0:T(8,128)} dynamic-update-slice(f32[18,130,320]{1,2,0:T(8,128)} %fusion.30, f32[16,128,320]{1,2,0:T(8,128)} %slice_add_fusion.4, s32[]{:T(128)} %constant.291.clone.1, s32[]{:T(128)} %constant.291.clone.1, s32[]{:T(128)} %constant.286.clone.1) | dynamic-update-slice | bytes 5242884 | tf_op jit(solution)/shard_map/scatter-add | solution.py:56
  85.1 5.0 slice_add_fusion.3
  90.1 14.0 %scatter-add.39 = f32[18,130,320]{1,2,0:T(8,128)} dynamic-update-slice(f32[18,130,320]{1,2,0:T(8,128)} %scatter-add.36, f32[16,128,320]{1,2,0:T(8,128)} %slice_add_fusion.3, s32[]{:T(128)} %constant.291.clone.1, s32[]{:T(128)} %constant.287.clone.1, s32[]{:T(128)} %constant.286.clone.1) | dynamic-update-slice | bytes 5242884 | tf_op jit(solution)/shard_map/scatter-add | solution.py:56
  104.1 4.3 fusion.29
  108.4 5.0 slice_add_fusion.1
  113.4 14.0 %scatter-add.41 = f32[18,130,320]{1,2,0:T(8,128)} dynamic-update-slice(f32[18,130,320]{1,2,0:T(8,128)} %fusion.29, f32[16,128,320]{1,2,0:T(8,128)} %slice_add_fusion.1, s32[]{:T(128)} %constant.287.clone.1, s32[]{:T(128)} %constant.291.clone.1, s32[]{:T(128)} %constant.286.clone.1) | dynamic-update-slice | bytes 5242884 | tf_op jit(solution)/shard_map/scatter-add | solution.py:56
  127.4 5.0 slice_add_fusion
  132.4 14.1 %scatter-add.44 = f32[18,130,320]{1,2,0:T(8,128)} dynamic-update-slice(f32[18,130,320]{1,2,0:T(8,128)} %scatter-add.41, f32[16,128,320]{1,2,0:T(8,128)} %slice_add_fusion, s32[]{:T(128)} %constant.287.clone.1, s32[]{:T(128)} %constant.287.clone.1, s32[]{:T(128)} %constant.286.clone.1) | dynamic-update-slice | bytes 5242884 | tf_op jit(solution)/shard_map/scatter-add | solution.py:56
  146.5 5.2 fusion.27
  169.5 5.7 reshape.492
  175.2 31.6 %concatenate.30 = f32[950272]{0:T(1024)} concatenate(f32[921600]{0:T(1024)} %reshape.492, f32[320]{0:T(512)S(1)} %convert_reduce_fusion.1, f32[320]{0:T(512)S(1)} %get-tuple-element.116, f32[320]{0:T(512)S(1)} %get-tuple-element.118, f32[27712]{0:T(1024)S(1)} %broadcast_in_dim.32), dimensions={0} | concatenate | bytes 7602176 | tf_op jit(solution)/shard_map/concatenate | solution.py:71
  206.8 4.6 reshape.493
  211.5 127.1 %reduce-scatter.2.cloned.1.call-done = f32[8,3712]{1,0:T(8,128)} async-done(((f32[8,118784]{1,0:T(8,128)}), f32[8,3712]{1,0:T(8,128)}) %reduce-scatter.2.cloned.1.call-update) | async-done | bytes 118800 | tf_op jit(solution)/shard_map/reduce_scatter | solution.py:75
  339.3 77.4 %all-reduce.5.cloned.1.call-done = f32[8,3712]{1,0:T(8,128)} async-done(((f32[8,3712]{1,0:T(8,128)}), f32[8,3712]{1,0:T(8,128)}) %all-reduce.5.cloned.1.call-update) | async-done | bytes 118800
  418.9 79.0 %psum.7 = f32[]{:T(128)} all-reduce(f32[]{:T(128)} %multiply_reduce_fusion.1), channel_id=1, replica_groups=mesh['grp'=8,'dp'=32] {'grp','dp'}, use_global_device_ids=true, to_apply=%region_15.16 | all-reduce | flops 1 | bytes 8 | tf_op jit(solution)/shard_map/psum | solution.py:77
  501.9 4.0 fusion.211
  509.5 402.4 %all-gather.3.cloned.1.call-done = bf16[256,1,3712]{2,1,0:T(2,128)(2,1)} async-done(((bf16[1,1,3712]{2,1,0:T(2,128)(2,1)}), bf16[256,1,3712]{2,1,0:T(2,128)(2,1)}) %all-gather.3.cloned.1.call-update) | async-done | bytes 1900560 | tf_op jit(solution)/shard_map/all_gather | solution.py:85
  912.0 12.0 %reduce.34 = bf16[256,3712]{1,0:T(8,128)(2,1)S(1)} reduce(bf16[256,1,3712]{2,1,0:T(2,128)(2,1)} %all-gather.3.cloned.1.call-done, bf16[]{:T(256)} %constant.319), dimensions={1}, to_apply=%all-gather.reduce_sub_computation | reduce | bytes 3801090 | tf_op jit(solution)/shard_map/all_gather | solution.py:85
  (78 shorter events, 49.2 us)
Async XLA Ops:
  7.2 3.5 copy-start
  7.2 3.7 copy-start.1
  7.2 331.4 %reduce-scatter.2.cloned.1.call-start = ((), (), s32[]{:S(2)}) async-start(), calls=%async_computation.1 | async-start | bytes 3919872 | tf_op jit(solution)/shard_map/reduce_scatter | solution.py:75
  18.6 4.6 copy-start.8
  132.4 14.1 %copy-start.6 = (f32[320]{0:T(512)S(1)}, f32[320]{0:T(512)}, u32[]{:S(2)}) copy-start(f32[320]{0:T(512)} %param.29) | copy-start | bytes 3844
  132.4 14.1 %copy-start.7 = (f32[320]{0:T(512)S(1)}, f32[320]{0:T(512)}, u32[]{:S(2)}) copy-start(f32[320]{0:T(512)} %param.30) | copy-start | bytes 3844
  151.7 2.6 copy-start.2
  211.4 127.3 %copy-start.9 = (u32[256]{0:T(256)S(1)}, u32[256]{0:T(256)}, u32[]{:S(2)}) copy-start(u32[256]{0:T(256)} %constant.316) | copy-start | bytes 3076
  211.4 288.8 %copy-start.3 = (f32[3712]{0:T(1024)S(1)}, f32[3712]{0:T(1024)}, u32[]{:S(2)}) copy-start(f32[3712]{0:T(1024)} %param.31) | copy-start | bytes 44548
  211.4 288.8 %copy-start.4 = (f32[3712]{0:T(1024)S(1)}, f32[3712]{0:T(1024)}, u32[]{:S(2)}) copy-start(f32[3712]{0:T(1024)} %param.33) | copy-start | bytes 44548
  211.4 288.8 %copy-start.5 = (f32[3712]{0:T(1024)S(1)}, f32[3712]{0:T(1024)}, u32[]{:S(2)}) copy-start(f32[3712]{0:T(1024)} %param.32) | copy-start | bytes 44548
  211.5 205.2 %all-reduce.5.cloned.1.call-start = ((), (), s32[]{:S(2)}) async-start(), calls=%async_computation.3 | async-start | bytes 237568
  338.6 573.3 %all-gather.3.cloned.1.call-start = ((), (), s32[]{:S(2)}) async-start(), calls=%async_computation.2 | async-start | bytes 3815936 | tf_op jit(solution)/shard_map/all_gather | solution.py:85
Sparse Core Ops, SparseCore 0:
  211.6 126.9 reduce-scatter.1
  341.2 75.4 all-reduce.4
  501.6 410.2 all-gather.2
where the time goes:
time: 945 us; the launch traced here: 940 us
  waiting for transfers between devices  607 us (64%)
  local copies, waits for them, and re-layouts  151 us (16%)
  blocking collectives  79 us (8%)
  matrix products  57 us (6%)
  other arithmetic  31 us (3%)
  between operations  14.7 us (2%)
    all_gather x1, waiting for transfers between devices, on_device(): whole = lax.all_gather(rounded, ('grp', 'dp'), axis=0, tiled=True)  402 us
    reduce_scatter x1, waiting for transfers between devices, on_device(): within = lax.psum_scatter(grouped, 'dp', scatter_dimension=1, tiled=True)  127 us
    scatter-add x7, local copies, waits for them, and re-layouts, local_grads(): padded_grad = padded_grad.at[tap_row:tap_row + height, tap_col:tap_col +...  90.2 us
    psum x1, blocking collectives, on_device(): norm_total = lax.psum(jnp.sum(summed * summed), ('grp', 'dp'))  79 us
    unnamed x4, waiting for transfers between devices  77.5 us
    dot_general x9, matrix products, local_grads(): lax.dot_general(cot_rows, weight[tap_row, tap_col], (((1,), (1,)), ((), (...  41.9 us
    concatenate x1, local copies, waits for them, and re-layouts, on_device(): jnp.concatenate([flat_grad, jnp.zeros((flat_len - flat_grad.shape[0],), j...  31.6 us
  transfers between devices with their start and end apart: 3, of which 3 were waited for; matrix products, arithmetic and copies ran while one was open for 1% of the time, Pallas kernels for 0%

commit v1 on v0

v1 whole, which is shorter than its diff:
```python
import functools

import jax
import jax.numpy as jnp
from jax import lax
from jax.experimental import pallas as pl
from jax.experimental.pallas import tpu as pltpu
from jax.sharding import PartitionSpec as P

GROUPS = 32
LANES = 128
PAD_ROWS = 32

norm_epsilon = 1e-05
beta_first = 0.9
beta_second = 0.999
adam_epsilon = 1e-08
learn_rate = 0.001
weight_decay = 0.01
clip_limit = 1.0
correct_first = 1.0
correct_second = 0.6323045752290363

MESH = pl.DeviceIdType.MESH
VMEM_LIMIT = 60 * 1024 * 1024


def swap_halves(block):
    return pltpu.roll(block, LANES // 2, axis=1)


def lower_half(shape):
    return lax.broadcasted_iota(jnp.int32, shape, 1) < LANES // 2


def grads_kernel(
    shard_rows,
    x_ref,
    cot_ref,
    w_ref,
    gain_ref,
    shift_ref,
    gin_ref,
    own_ref,
    other_ref,
    act3,
    cot3,
    wcat,
    kgrad,
    flat,
    normed_s,
    dact_s,
    gact,
):
    height, channels, width = x_ref.shape
    count = height * width * (channels // GROUPS)
    core = lax.axis_index("dp") % 2
    f32, bf16 = jnp.float32, jnp.bfloat16

    row_id = lax.broadcasted_iota(jnp.int32, (channels, channels), 0)
    col_id = lax.broadcasted_iota(jnp.int32, (channels, channels), 1)
    eye = (row_id == col_id).astype(f32)
    per = 1.0 / (channels // GROUPS)
    row_group = jnp.floor((row_id.astype(f32) + 0.5) * per)
    col_group = jnp.floor((col_id.astype(f32) + 0.5) * per)
    same_group = (row_group == col_group).astype(f32)

    def group_mean(block):
        mixed = jnp.dot(
            same_group, block, precision=lax.Precision.HIGHEST, preferred_element_type=f32
        )
        return jnp.sum(mixed, axis=1, keepdims=True) * (1.0 / count)

    def as_column(row):
        return jnp.sum(eye * row, axis=1, keepdims=True)

    def as_row(column):
        return jnp.sum(eye * column, axis=0, keepdims=True)

    gain = as_column(gain_ref[...])
    shift = as_column(shift_ref[...])

    zero_block = jnp.zeros((channels, width), f32)
    total = lax.fori_loop(
        0, height, lambda r, s: s + x_ref[r].astype(f32), zero_block
    )
    centre = group_mean(total)

    def spread_step(r, s):
        centred = x_ref[r].astype(f32) - centre
        return s + centred * centred

    spread = group_mean(lax.fori_loop(0, height, spread_step, zero_block))
    rstd = lax.rsqrt(spread + norm_epsilon)

    lane = lax.broadcasted_iota(jnp.int32, (channels, width), 1)
    zero_bf = jnp.zeros((channels, width), bf16)
    act3[0:channels, 0:width] = zero_bf
    act3[2 * channels : 3 * channels, (height - 1) * width : height * width] = zero_bf
    cot3[3 * channels :, :] = jnp.zeros((cot3.shape[0] - 3 * channels, cot3.shape[1]), bf16)

    bias_total = zero_block
    for r in range(height):
        normed = (x_ref[r].astype(f32) - centre) * rstd
        pre = normed * gain + shift
        sig = 1.0 / (1.0 + jnp.exp(-pre))
        act = (pre * sig).astype(bf16)
        normed_s[r] = normed
        dact_s[r] = sig * (1.0 + pre * (1.0 - sig))
        for i in range(3):
            dest = r - i + 1
            if 0 <= dest < height:
                act3[i * channels : (i + 1) * channels, dest * width : (dest + 1) * width] = act
        cot = cot_ref[r].astype(f32)
        bias_total = bias_total + cot
        place = slice(r * width, (r + 1) * width)
        ahead = jnp.where(lane < width - 1, pltpu.roll(cot, width - 1, axis=1), 0.0)
        behind = jnp.where(lane > 0, pltpu.roll(cot, 1, axis=1), 0.0)
        cot3[0:channels, place] = ahead.astype(bf16)
        cot3[channels : 2 * channels, place] = cot_ref[r]
        cot3[2 * channels : 3 * channels, place] = behind.astype(bf16)

    def kernel_step(n, carry):
        start = pl.multiple_of(n * 256, 256)
        block = lax.dot_general(
            act3[...],
            cot3[pl.ds(start, 256), :],
            (((1,), (1,)), ((), ())),
            preferred_element_type=f32,
        )
        kgrad[2 * n] = block[:, :LANES]
        kgrad[2 * n + 1] = block[:, LANES:]
        return carry

    lax.fori_loop(0, cot3.shape[0] // 256, kernel_step, 0)

    wcat[...] = jnp.zeros_like(wcat)
    for i in range(3):
        for j in range(3):
            wcat[i * channels : (i + 1) * channels, j * channels : (j + 1) * channels] = w_ref[
                3 * i + j
            ]
    gact[...] = jnp.zeros_like(gact)

    def back_step(n, carry):
        start = pl.multiple_of(n * 256, 256)
        block = jnp.dot(wcat[...], cot3[:, pl.ds(start, 256)], preferred_element_type=f32)
        for i in range(3):
            for h in range(2):
                gact[2 * n + h + i] += block[
                    i * channels : (i + 1) * channels, h * width : (h + 1) * width
                ]
        return carry

    lax.fori_loop(0, height // 2, back_step, 0)

    def sums_step(r, carry):
        shift_sum, gain_sum = carry
        dpre = gact[r + 1] * dact_s[r]
        gact[r + 1] = dpre
        return shift_sum + dpre, gain_sum + dpre * normed_s[r]

    shift_sum, gain_sum = lax.fori_loop(0, height, sums_step, (zero_block, zero_block))
    mean_grad = group_mean(shift_sum * gain)
    mean_cross = group_mean(gain_sum * gain)

    def input_step(r, carry):
        slope = gact[r + 1] * gain
        gin_ref[r] = (rstd * (slope - mean_grad - normed_s[r] * mean_cross)).astype(bf16)
        return carry

    lax.fori_loop(0, height, input_step, 0)

    half = channels // 2
    low = lower_half((half, LANES))
    flat_rows = flat.shape[0]
    for i in range(3):
        for j in range(3):
            first = (j * channels) // LANES
            even = [kgrad[first + b, pl.ds(i * channels, half, stride=2), :] for b in range(3)]
            odd = [kgrad[first + b, pl.ds(i * channels + 1, half, stride=2), :] for b in range(3)]
            if j == 1:
                even_r = [swap_halves(e) for e in even]
                pieces = [
                    jnp.where(low, even_r[0], even_r[1]),
                    jnp.where(low, even_r[1], even_r[2]),
                    jnp.where(low, even_r[2], odd[0]),
                    odd[1],
                    odd[2],
                ]
            else:
                odd_r = [swap_halves(o) for o in odd]
                pieces = [
                    even[0],
                    even[1],
                    jnp.where(low, even[2], odd_r[0]),
                    jnp.where(low, odd_r[0], odd_r[1]),
                    jnp.where(low, odd_r[1], odd_r[2]),
                ]
            base = (3 * i + j) * (channels * channels // LANES)
            for b in range(5):
                flat[pl.ds(base + b, half, stride=5), :] = pieces[b]

    used = 9 * channels * channels // LANES
    bias_row = as_row(jnp.sum(bias_total, axis=1, keepdims=True))
    gain_row = as_row(jnp.sum(gain_sum, axis=1, keepdims=True))
    shift_row = as_row(jnp.sum(shift_sum, axis=1, keepdims=True))
    flat[used:flat_rows, :] = jnp.zeros((flat_rows - used, LANES), f32)
    flat[used : used + 1, :] = bias_row[:, 0:128]
    flat[used + 1 : used + 2, :] = bias_row[:, 128:256]
    flat[used + 2 : used + 3, 0:64] = bias_row[:, 256:320]
    flat[used + 2 : used + 3, 64:128] = gain_row[:, 0:64]
    flat[used + 3 : used + 4, :] = gain_row[:, 64:192]
    flat[used + 4 : used + 5, :] = gain_row[:, 192:320]
    flat[used + 5 : used + 6, :] = shift_row[:, 0:128]
    flat[used + 6 : used + 7, :] = shift_row[:, 128:256]
    flat[used + 7 : used + 8, 0:64] = shift_row[:, 256:320]

    def shard_step(q, carry):
        own_ref[q] = flat[pl.ds((2 * q + core) * shard_rows, PAD_ROWS), :]
        other_ref[q] = flat[pl.ds((2 * q + 1 - core) * shard_rows, PAD_ROWS), :].astype(bf16)
        return carry

    lax.fori_loop(0, own_ref.shape[0], shard_step, 0)


def sample_grads(x, cot, weight, gain, shift, shards, shard_rows):
    height, channels, width = x.shape
    f32, bf16 = jnp.float32, jnp.bfloat16
    wide = -(-3 * channels // 256) * 256
    flat_rows = shards * shard_rows + PAD_ROWS
    return pl.pallas_call(
        functools.partial(grads_kernel, shard_rows),
        out_shape=(
            jax.ShapeDtypeStruct(x.shape, bf16),
            jax.ShapeDtypeStruct((shards // 2, PAD_ROWS, LANES), f32),
            jax.ShapeDtypeStruct((shards // 2, PAD_ROWS, LANES), bf16),
        ),
        scratch_shapes=[
            pltpu.VMEM((3 * channels, height * width), bf16),
            pltpu.VMEM((wide, height * width), bf16),
            pltpu.VMEM((3 * channels, wide), bf16),
            pltpu.VMEM((wide // LANES, 3 * channels, LANES), f32),
            pltpu.VMEM((flat_rows, LANES), f32),
            pltpu.VMEM((height, channels, width), f32),
            pltpu.VMEM((height, channels, width), f32),
            pltpu.VMEM((height + 2, channels, width), f32),
        ],
        compiler_params=pltpu.CompilerParams(vmem_limit_bytes=VMEM_LIMIT),
    )(x, cot, weight.reshape(9, channels, channels), gain[None], shift[None])


def update_kernel(
    split_rows,
    own_ref,
    other_ref,
    master_ref,
    first_ref,
    second_ref,
    gath,
    new_master_ref,
    new_first_ref,
    new_second_ref,
    recv1,
    send2,
    recv2,
    acc,
    recv3,
    norm_line,
    norm_plane,
    s1,
    r1,
    s2,
    r2,
    s3,
    r3,
    sl,
    rl,
    sp,
    rp,
    sa,
    ra,
    sb,
    rb,
    sc,
    rc,
):
    f32, bf16 = jnp.float32, jnp.bfloat16
    plane, depth = own_ref.shape[0], own_ref.shape[1]
    line = 2 * depth
    grp, dp = lax.axis_index("grp"), lax.axis_index("dp")
    p = grp * split_rows + dp // line
    spot = dp % line
    z, core = spot // 2, spot % 2
    shard_rows = master_ref.shape[0]

    def device(p_, spot_):
        return (p_ // split_rows, (p_ % split_rows) * line + spot_)

    def in_plane(t):
        return device((p + t) % plane, spot)

    def in_line(t):
        return device(p, (spot + t) % line)

    def in_depth(t):
        return device(p, ((z + t) % depth) * 2 + core)

    partner = device(p, z * 2 + 1 - core)

    def copy(src, dst, send, recv, target):
        return pltpu.make_async_remote_copy(
            src_ref=src,
            dst_ref=dst,
            send_sem=send,
            recv_sem=recv,
            device_id=target,
            device_id_type=MESH,
        )

    def loop(lo, hi, body):
        def step(t, carry):
            body(t)
            return carry

        lax.fori_loop(lo, hi, step, 0)

    barrier = pltpu.get_barrier_semaphore()
    loop(1, plane, lambda t: pl.semaphore_signal(barrier, inc=1, device_id=in_plane(t), device_id_type=MESH))
    loop(1, line, lambda t: pl.semaphore_signal(barrier, inc=1, device_id=in_line(t), device_id_type=MESH))
    pl.semaphore_wait(barrier, plane + line - 2)

    def pair(t):
        q = (p + t) % plane
        return copy(other_ref.at[q], recv1.at[q], s1.at[t], r1.at[t], partner)

    loop(1, plane, lambda t: pair(t).start())
    pair(0).start()

    def across(t):
        return copy(send2.at[t], recv2.at[t], s2.at[t], r2.at[t], in_plane(t))

    def across_start(t):
        pair(t).wait_recv()
        q = (p + t) % plane
        send2[t] = (own_ref[q] + recv1[q].astype(f32)).astype(bf16)
        across(t).start()

    loop(1, plane, across_start)
    pair(0).wait_recv()
    acc[...] = own_ref[p] + recv1[p].astype(f32)

    def across_take(t):
        across(t).wait_recv()
        acc[...] += recv2[t].astype(f32)

    loop(1, plane, across_take)

    def along(t):
        return copy(acc.at[(z + t) % depth], recv3.at[t], s3.at[t], r3.at[t], in_depth(t))

    loop(1, depth, lambda t: along(t).start())
    recv3[0] = acc[z]
    loop(1, depth, lambda t: along(t).wait_recv())
    summed = recv3[0]
    for t in range(1, depth):
        summed = summed + recv3[t]
    live = lax.broadcasted_iota(jnp.int32, summed.shape, 0) < shard_rows
    summed = jnp.where(live, summed, 0.0)

    squares = summed * summed
    norm_line[0] = squares[0:8] + squares[8:16] + squares[16:24] + squares[24:32]

    def line_copy(t):
        return copy(norm_line.at[0], norm_line.at[t], sl.at[t], rl.at[t], in_line(t))

    loop(1, line, lambda t: line_copy(t).start())
    loop(1, line, lambda t: line_copy(t).wait_recv())
    part = norm_line[0]
    for t in range(1, line):
        part = part + norm_line[t]
    norm_plane[0] = part

    def plane_copy(t):
        return copy(norm_plane.at[0], norm_plane.at[t], sp.at[t], rp.at[t], in_plane(t))

    loop(1, plane, lambda t: plane_copy(t).start())
    loop(1, plane, lambda t: plane_copy(t).wait_recv())
    part = norm_plane[0]
    for t in range(1, plane):
        part = part + norm_plane[t]
    norm_total = jnp.sum(jnp.sum(part, axis=1, keepdims=True), axis=0, keepdims=True)

    clip = jnp.minimum(1.0, clip_limit / (jnp.sqrt(norm_total) + 1e-06))
    clipped = (clip * summed)[0:shard_rows]
    new_first = beta_first * first_ref[...] + (1.0 - beta_first) * clipped
    new_second = beta_second * second_ref[...] + (1.0 - beta_second) * clipped * clipped
    step_dir = new_first / correct_first / (jnp.sqrt(new_second / correct_second) + adam_epsilon)
    master = master_ref[...]
    new_master = master - learn_rate * (step_dir + weight_decay * master)
    new_master_ref[...] = new_master
    new_first_ref[...] = new_first
    new_second_ref[...] = new_second
    recv3[0, 0:shard_rows] = new_master
    gath[core, p, z] = recv3[0].astype(bf16)

    def gather_depth(t):
        mine = gath.at[core, p, z]
        return copy(mine, mine, sa.at[t], ra.at[t], in_depth(t))

    def gather_plane(t):
        mine = gath.at[core, p]
        return copy(mine, mine, sb.at[t], rb.at[t], in_plane(t))

    def gather_core(t):
        block = gath.at[core, (p + plane - t) % plane]
        return copy(block, block, sc.at[t], rc.at[t], partner)

    loop(1, depth, lambda t: gather_depth(t).start())
    loop(1, depth, lambda t: gather_depth(t).wait_recv())
    loop(1, plane, lambda t: gather_plane(t).start())
    gather_core(0).start()

    def pass_on(t):
        gather_plane(t).wait_recv()
        gather_core(t).start()

    loop(1, plane, pass_on)
    loop(0, plane, lambda t: gather_core(t).wait_recv())

    loop(0, plane, lambda t: pair(t).wait_send())
    loop(1, plane, lambda t: across(t).wait_send())
    loop(1, depth, lambda t: along(t).wait_send())
    loop(1, line, lambda t: line_copy(t).wait_send())
    loop(1, plane, lambda t: plane_copy(t).wait_send())
    loop(1, depth, lambda t: gather_depth(t).wait_send())
    loop(1, plane, lambda t: gather_plane(t).wait_send())
    loop(0, plane, lambda t: gather_core(t).wait_send())


def reduce_and_update(own, other, master, first, second, plane, depth, split_rows):
    f32, bf16 = jnp.float32, jnp.bfloat16
    line = 2 * depth
    own = own.reshape(plane, depth, PAD_ROWS, LANES)
    other = other.reshape(plane, depth, PAD_ROWS, LANES)
    shard = jax.ShapeDtypeStruct(master.shape, f32)
    dma = lambda n: pltpu.SemaphoreType.DMA((n,))
    return pl.pallas_call(
        functools.partial(update_kernel, split_rows),
        out_shape=(
            jax.ShapeDtypeStruct((2, plane, depth, PAD_ROWS, LANES), bf16),
            shard,
            shard,
            shard,
        ),
        in_specs=[pl.BlockSpec(memory_space=pltpu.VMEM)] * 5,
        out_specs=[pl.BlockSpec(memory_space=pltpu.VMEM)] * 4,
        scratch_shapes=[
            pltpu.VMEM((plane, depth, PAD_ROWS, LANES), bf16),
            pltpu.VMEM((plane, depth, PAD_ROWS, LANES), bf16),
            pltpu.VMEM((plane, depth, PAD_ROWS, LANES), bf16),
            pltpu.VMEM((depth, PAD_ROWS, LANES), f32),
            pltpu.VMEM((depth, PAD_ROWS, LANES), f32),
            pltpu.VMEM((line, 8, LANES), f32),
            pltpu.VMEM((plane, 8, LANES), f32),
        ]
        + [dma(n) for n in (plane, plane, plane, plane, depth, depth, line, line)]
        + [dma(n) for n in (plane, plane, depth, depth, plane, plane, plane, plane)],
        compiler_params=pltpu.CompilerParams(
            collective_id=0, has_side_effects=True, vmem_limit_bytes=VMEM_LIMIT
        ),
    )(own, other, master, first, second)


def unpack_kernel(shard_rows, gath, weight_ref, bias_ref, gain_ref, shift_ref, flat, rows):
    f32, bf16 = jnp.float32, jnp.bfloat16
    plane, depth = gath.shape[1], gath.shape[2]
    total, channels = weight_ref.shape

    def shard_step(q, carry):
        for core in range(2):
            block = gath[core, q // depth, q % depth].astype(f32)
            flat[pl.ds((2 * q + core) * shard_rows, PAD_ROWS), :] = block
        return carry

    lax.fori_loop(0, plane * depth, shard_step, 0)

    half = channels // 2
    low = lower_half((half, LANES))
    five = channels * channels // LANES

    def rows_step(n, carry):
        piece = [flat[pl.ds(n * five + b, half, stride=5), :] for b in range(5)]
        turned = [swap_halves(piece[b]) for b in range(2, 5)]
        even = [piece[0], piece[1], piece[2]]
        odd = [
            jnp.where(low, turned[0], turned[1]),
            jnp.where(low, turned[1], turned[2]),
            turned[2],
        ]
        for b in range(3):
            rows[b, pl.ds(0, half, stride=2), :] = even[b]
            rows[b, pl.ds(1, half, stride=2), :] = odd[b]
        place = pl.ds(pl.multiple_of(n * channels, channels), channels)
        weight_ref[place, 0:128] = rows[0].astype(bf16)
        weight_ref[place, 128:256] = rows[1].astype(bf16)
        weight_ref[place, 256:channels] = rows[2, :, 0 : channels - 256].astype(bf16)
        return carry

    lax.fori_loop(0, total // channels, rows_step, 0)

    used = total * channels // LANES
    tail = [flat[used + b : used + b + 1, :].astype(bf16) for b in range(8)]
    bias_ref[:, 0:128] = tail[0]
    bias_ref[:, 128:256] = tail[1]
    bias_ref[:, 256:320] = tail[2][:, 0:64]
    gain_ref[:, 0:64] = tail[2][:, 64:128]
    gain_ref[:, 64:192] = tail[3]
    gain_ref[:, 192:320] = tail[4]
    shift_ref[:, 0:128] = tail[5]
    shift_ref[:, 128:256] = tail[6]
    shift_ref[:, 256:320] = tail[7][:, 0:64]


def unpack(gath, channels, shard_rows):
    bf16, f32 = jnp.bfloat16, jnp.float32
    shards = 2 * gath.shape[1] * gath.shape[2]
    row = jax.ShapeDtypeStruct((1, channels), bf16)
    return pl.pallas_call(
        functools.partial(unpack_kernel, shard_rows),
        out_shape=(jax.ShapeDtypeStruct((9 * channels, channels), bf16), row, row, row),
        scratch_shapes=[
            pltpu.VMEM((shards * shard_rows + PAD_ROWS, LANES), f32),
            pltpu.VMEM((3, channels, LANES), f32),
        ],
        compiler_params=pltpu.CompilerParams(vmem_limit_bytes=VMEM_LIMIT),
    )(gath)


def on_device(latents, cotangent, weight, gain, shift, master, first_moment, second_moment):
    groups, owners = lax.axis_size("grp"), lax.axis_size("dp")
    channels = weight.shape[2]
    split_rows = 2
    depth = owners // (2 * split_rows)
    plane = groups * split_rows
    shard_rows = master.shape[0] // LANES
    x = jnp.transpose(latents[0], (0, 2, 1))
    cot = jnp.transpose(cotangent[0], (0, 2, 1))
    grad_in, own, other = sample_grads(x, cot, weight, gain, shift, groups * owners, shard_rows)
    shaped = [a.reshape(shard_rows, LANES) for a in (master, first_moment, second_moment)]
    gath, new_master, new_first, new_second = reduce_and_update(
        own, other, *shaped, plane, depth, split_rows
    )
    new_weight, new_bias, new_gain, new_shift = unpack(gath, channels, shard_rows)
    return (
        jnp.transpose(grad_in, (0, 2, 1))[None],
        new_weight.reshape(weight.shape),
        new_bias.reshape(channels),
        new_gain.reshape(channels),
        new_shift.reshape(channels),
        new_master.reshape(-1),
        new_first.reshape(-1),
        new_second.reshape(-1),
    )


def solution(mesh):
    split = ("grp", "dp")
    whole = P(split, None, None, None)
    in_specs = (whole, whole, P(), P(), P(), P(split), P(split), P(split))
    out_specs = (whole, P(), P(), P(), P(), P(split), P(split), P(split))
    return jax.shard_map(
        on_device, mesh=mesh, in_specs=in_specs, out_specs=out_specs, check_vma=False
    )
```

time: 945 us -> 113 us (0.12)
  waiting for transfers between devices: 607 us -> 0 us
  local copies, waits for them, and re-layouts: 151 us -> 4.32 us
  Pallas kernels: 0 us -> 103 us
  blocking collectives: 79 us -> 0 us
  matrix products: 57 us -> 0 us
  other arithmetic: 31 us -> 3.78 us
  between operations: 14.7 us -> 0.67 us
    all_gather x1 -> x0, waiting for transfers between devices: 402 us -> none  [on_device(): whole = lax.all_gather(rounded, ('grp', 'dp'), axis=0, tiled=True)]
    reduce_scatter x1 -> x0, waiting for transfers between devices: 127 us -> none  [on_device(): within = lax.psum_scatter(grouped, 'dp', scatter_dimension=1, tiled=True)]
    pallas_call x0 -> x3, Pallas kernels: none -> 103 us  [the longest x1 72.2 us: reduce_and_update(): pl.pallas_call(functools.partial(update_kernel, split_rows), out_shape=(j...]
    scatter-add x7 -> x0, local copies, waits for them, and re-layouts: 90.2 us -> none  [local_grads(): padded_grad = padded_grad.at[tap_row:tap_row + height, tap_col:tap_col +...]
    psum x1 -> x0, blocking collectives: 79 us -> none  [on_device(): norm_total = lax.psum(jnp.sum(summed * summed), ('grp', 'dp'))]
    unnamed x4 -> x0, waiting for transfers between devices: 77.5 us -> none
    dot_general x18 -> x0, matrix products: 57 us -> none  [the longest x9 41.9 us: local_grads(): lax.dot_general(cot_rows, weight[tap_row, tap_col], (((1,), (1,)), ((), (...]
    concatenate x1 -> x0, local copies, waits for them, and re-layouts: 31.6 us -> none  [on_device(): jnp.concatenate([flat_grad, jnp.zeros((flat_len - flat_grad.shape[0],), j...]
  transfers between devices with their start and end apart: 3 -> 0, of which waited for: 3 -> 0; matrix products, arithmetic and copies ran while one was open for 1% -> 0% of each run, Pallas kernels for 0% -> 0%
where the time goes in v1:
time: 113 us; the launch traced here: 112 us
  Pallas kernels  103 us (91%)
  local copies, waits for them, and re-layouts  4.32 us (4%)
  other arithmetic  3.78 us (3%)
    pallas_call x1, Pallas kernels, reduce_and_update(): pl.pallas_call(functools.partial(update_kernel, split_rows), out_shape=(j...  72.2 us
    pallas_call x1, Pallas kernels, sample_grads(): pl.pallas_call(functools.partial(grads_kernel, shard_rows), out_shape=(ja...  25.2 us
    pallas_call x1, Pallas kernels, unpack(): pl.pallas_call(functools.partial(unpack_kernel, shard_rows), out_shape=(j...  6.06 us
    pallas_call x3, other arithmetic, unpack(): pl.pallas_call(functools.partial(unpack_kernel, shard_rows), out_shape=(j...  3.78 us

profile of v1, /device:TPU:1, one launch (start us, length us, event | category | flops | bytes accessed | tf_op | source)
XLA Modules:
  0.0 112.3 jit_solution(8126541685939474576)
XLA Ops:
  0.6 1.2 %broadcast_in_dim.9.gain_ref = f32[1,320]{1,0:T(1,128)} reshape(f32[320]{0:T(512)} %param.11) | data formatting | bytes 2560 | tf_op jit(solution)/shard_map/broadcast_in_dim | solution.py:250
  1.9 1.2 %broadcast_in_dim.10.shift_ref = f32[1,320]{1,0:T(1,128)} reshape(f32[320]{0:T(512)} %param.12) | data formatting | bytes 2560 | tf_op jit(solution)/shard_map/broadcast_in_dim | solution.py:250
  3.1 25.2 %shard_map.143 = (bf16[16,320,128]{2,1,0:T(8,128)(2,1)}, f32[128,32,128]{2,1,0:T(8,128)}, bf16[128,32,128]{2,1,0:T(8,128)(2,1)}) custom-call(bf16[16,320,128]{2,1,0:T(8,128)(2,1)} %bitcast.21, bf16[16,320,128]{2,1,0:T(8,128)(2,1)} %bitcast.22, bf16[9,320,320]{2,1,0:T(8,128)(2,1)} %bitcast.19, f32[1,320]{1,0:T(1,128)} %broadcast_in_dim.9.gain_ref, ...), custom_call_target="tpu_custom_call" | custom-call | tf_op jit(solution)/shard_map/pallas_call | solution.py:232
  28.3 72.2 %shard_map.144 = (bf16[2,16,8,32,128]{4,3,2,1,0:T(8,128)(2,1)}, f32[29,128]{1,0:T(8,128)}, f32[29,128]{1,0:T(8,128)}, f32[29,128]{1,0:T(8,128)}) custom-call(f32[16,8,32,128]{3,2,1,0:T(8,128)} %bitcast.20, bf16[16,8,32,128]{3,2,1,0:T(8,128)(2,1)} %bitcast.23, f32[29,128]{1,0:T(8,128)} %bitcast.24, f32[29,128]{1,0:T(8,128)} %bitcast.25, f32[29,128]{1,0:T(8,128)} %bitcast.26), custom_call_target="tpu_custom_call" | custom-call | tf_op jit(solution)/shard_map/pallas_call | solution.py:448
  100.6 0.0 copy-start.2
  100.6 0.0 copy-start.1
  100.6 0.0 copy-start
  100.6 6.1 %shard_map.145 = (bf16[2880,320]{1,0:T(8,128)(2,1)}, bf16[1,320]{1,0:T(2,128)(2,1)}, bf16[1,320]{1,0:T(2,128)(2,1)}, bf16[1,320]{1,0:T(2,128)(2,1)}) custom-call(bf16[2,16,8,32,128]{4,3,2,1,0:T(8,128)(2,1)} %get-tuple-element.22.gath), custom_call_target="tpu_custom_call" | custom-call | tf_op jit(solution)/shard_map/pallas_call | solution.py:529
  106.7 1.3 %reduce = bf16[320]{0:T(512)(128)(2,1)} reduce(bf16[1,320]{1,0:T(2,128)(2,1)} %get-tuple-element.24, bf16[]{:T(256)} %constant.5), dimensions={0}, to_apply=%get-tuple-element.24.reduce_sub_computation | reduce | bytes 1282 | tf_op jit(solution)/shard_map/pallas_call | solution.py:529
  107.9 1.3 %reduce.1 = bf16[320]{0:T(512)(128)(2,1)} reduce(bf16[1,320]{1,0:T(2,128)(2,1)} %get-tuple-element.25, bf16[]{:T(256)} %constant.5), dimensions={0}, to_apply=%get-tuple-element.25.reduce_sub_computation | reduce | bytes 1282 | tf_op jit(solution)/shard_map/pallas_call | solution.py:529
  109.2 1.3 %reduce.2 = bf16[320]{0:T(512)(128)(2,1)} reduce(bf16[1,320]{1,0:T(2,128)(2,1)} %get-tuple-element.26, bf16[]{:T(256)} %constant.5), dimensions={0}, to_apply=%get-tuple-element.26.reduce_sub_computation | reduce | bytes 1282 | tf_op jit(solution)/shard_map/pallas_call | solution.py:529
  110.4 0.0 copy-done.2
  110.4 0.6 copy.19
  111.0 0.0 copy-done.1
  111.1 0.6 copy.20
  111.7 0.0 copy-done
  111.7 0.6 copy.21
Async XLA Ops:
  100.6 9.9 %copy-start.2 = (f32[29,128]{1,0:T(8,128)S(1)}, f32[29,128]{1,0:T(8,128)}, u32[]{:S(2)}) copy-start(f32[29,128]{1,0:T(8,128)} %get-tuple-element.27) | copy-start | bytes 44548
  100.6 10.5 %copy-start.1 = (f32[29,128]{1,0:T(8,128)S(1)}, f32[29,128]{1,0:T(8,128)}, u32[]{:S(2)}) copy-start(f32[29,128]{1,0:T(8,128)} %get-tuple-element.28) | copy-start | bytes 44548
  100.6 11.1 %copy-start = (f32[29,128]{1,0:T(8,128)S(1)}, f32[29,128]{1,0:T(8,128)}, u32[]{:S(2)}) copy-start(f32[29,128]{1,0:T(8,128)} %get-tuple-element.29) | copy-start | bytes 44548

commit v2 on v1

--- a/solution.py
+++ b/solution.py
@@ -33,16 +33,26 @@
     return lax.broadcasted_iota(jnp.int32, shape, 1) < LANES // 2
 
 
-def grads_kernel(
-    shard_rows,
+def layer_kernel(
+    split_rows,
+    plane,
+    depth,
     x_ref,
     cot_ref,
-    w_ref,
+    w_hbm,
     gain_ref,
     shift_ref,
+    master_ref,
+    first_ref,
+    second_ref,
+    gin_hbm,
+    gath_hbm,
+    new_master_ref,
+    new_first_ref,
+    new_second_ref,
+    w_ref,
     gin_ref,
-    own_ref,
-    other_ref,
+    gath,
     act3,
     cot3,
     wcat,
@@ -51,11 +61,85 @@
     normed_s,
     dact_s,
     gact,
+    send1,
+    recv1,
+    send2,
+    recv2,
+    acc,
+    recv3,
+    norm_line,
+    norm_plane,
+    w_sem,
+    gin_sem,
+    s1,
+    r1,
+    s2,
+    r2,
+    s3,
+    r3,
+    sl,
+    rl,
+    sp,
+    rp,
+    sa,
+    ra,
+    sb,
+    rb,
+    sc,
+    rc,
+    out_sem,
 ):
+    f32, bf16 = jnp.float32, jnp.bfloat16
+    line = 2 * depth
+    grp, dp = lax.axis_index("grp"), lax.axis_index("dp")
+    p = grp * split_rows + dp // line
+    spot = dp % line
+    z, core = spot // 2, spot % 2
+    shard_rows = master_ref.shape[0]
+
+    def device(p_, spot_):
+        return (p_ // split_rows, (p_ % split_rows) * line + spot_)
+
+    def in_plane(t):
+        return device((p + t) % plane, spot)
+
+    def in_line(t):
+        return device(p, (spot + t) % line)
+
+    def in_depth(t):
+        return device(p, ((z + t) % depth) * 2 + core)
+
+    partner = device(p, z * 2 + 1 - core)
+
+    def copy(src, dst, send, recv, target):
+        return pltpu.make_async_remote_copy(
+            src_ref=src,
+            dst_ref=dst,
+            send_sem=send,
+            recv_sem=recv,
+            device_id=target,
+            device_id_type=MESH,
+        )
+
+    def loop(lo, hi, body):
+        def step(t, carry):
+            body(t)
+            return carry
+
+        lax.fori_loop(lo, hi, step, 0)
+
+    barrier = pltpu.get_barrier_semaphore()
+
+    def greet(target):
+        pl.semaphore_signal(barrier, inc=1, device_id=target, device_id_type=MESH)
+
+    loop(1, plane, lambda t: greet(in_plane(t)))
+    loop(1, line, lambda t: greet(in_line(t)))
+    w_copy = pltpu.make_async_copy(w_hbm, w_ref, w_sem)
+    w_copy.start()
+
     height, channels, width = x_ref.shape
     count = height * width * (channels // GROUPS)
-    core = lax.axis_index("dp") % 2
-    f32, bf16 = jnp.float32, jnp.bfloat16
 
     row_id = lax.broadcasted_iota(jnp.int32, (channels, channels), 0)
     col_id = lax.broadcasted_iota(jnp.int32, (channels, channels), 1)
@@ -77,8 +161,8 @@
     def as_row(column):
         return jnp.sum(eye * column, axis=0, keepdims=True)
 
-    gain = as_column(gain_ref[...])
-    shift = as_column(shift_ref[...])
+    gain = as_column(gain_ref[...].reshape(1, channels))
+    shift = as_column(shift_ref[...].reshape(1, channels))
 
     zero_block = jnp.zeros((channels, width), f32)
     total = lax.fori_loop(
@@ -133,43 +217,6 @@
         return carry
 
     lax.fori_loop(0, cot3.shape[0] // 256, kernel_step, 0)
-
-    wcat[...] = jnp.zeros_like(wcat)
-    for i in range(3):
-        for j in range(3):
-            wcat[i * channels : (i + 1) * channels, j * channels : (j + 1) * channels] = w_ref[
-                3 * i + j
-            ]
-    gact[...] = jnp.zeros_like(gact)
-
-    def back_step(n, carry):
-        start = pl.multiple_of(n * 256, 256)
-        block = jnp.dot(wcat[...], cot3[:, pl.ds(start, 256)], preferred_element_type=f32)
-        for i in range(3):
-            for h in range(2):
-                gact[2 * n + h + i] += block[
-                    i * channels : (i + 1) * channels, h * width : (h + 1) * width
-                ]
-        return carry
-
-    lax.fori_loop(0, height // 2, back_step, 0)
-
-    def sums_step(r, carry):
-        shift_sum, gain_sum = carry
-        dpre = gact[r + 1] * dact_s[r]
-        gact[r + 1] = dpre
-        return shift_sum + dpre, gain_sum + dpre * normed_s[r]
-
-    shift_sum, gain_sum = lax.fori_loop(0, height, sums_step, (zero_block, zero_block))
-    mean_grad = group_mean(shift_sum * gain)
-    mean_cross = group_mean(gain_sum * gain)
-
-    def input_step(r, carry):
-        slope = gact[r + 1] * gain
-        gin_ref[r] = (rstd * (slope - mean_grad - normed_s[r] * mean_cross)).astype(bf16)
-        return carry
-
-    lax.fori_loop(0, height, input_step, 0)
 
     half = channels // 2
     low = lower_half((half, LANES))
@@ -202,10 +249,88 @@
                 flat[pl.ds(base + b, half, stride=5), :] = pieces[b]
 
     used = 9 * channels * channels // LANES
+    flat[used:flat_rows, :] = jnp.zeros((flat_rows - used, LANES), f32)
+    last = used // (shard_rows * line)
+
+    def chunk(t):
+        return (p + t) % plane
+
+    def pair(t):
+        q = chunk(t)
+        return copy(send1.at[q], recv1.at[q], s1.at[t], r1.at[t], partner)
+
+    def pair_start(t):
+        q = chunk(t)
+        for k in range(depth):
+            row = ((q * depth + k) * 2 + 1 - core) * shard_rows
+            send1[q, k] = flat[pl.ds(row, PAD_ROWS), :].astype(bf16)
+        pair(t).start()
+
+    def early(body):
+        def step(t):
+            @pl.when(chunk(t) != last)
+            def _():
+                body(t)
+
+        return step
+
+    pl.semaphore_wait(barrier, plane + line - 2)
+    loop(1, plane, early(pair_start))
+    early(pair_start)(0)
+
+    w_copy.wait()
+    wcat[...] = jnp.zeros_like(wcat)
+    for i in range(3):
+        for j in range(3):
+            wcat[i * channels : (i + 1) * channels, j * channels : (j + 1) * channels] = w_ref[
+                3 * i + j
+            ]
+    gact[...] = jnp.zeros_like(gact)
+
+    def back_step(n, carry):
+        start = pl.multiple_of(n * 256, 256)
+        block = jnp.dot(wcat[...], cot3[:, pl.ds(start, 256)], preferred_element_type=f32)
+        for i in range(3):
+            for h in range(2):
+                gact[2 * n + h + i] += block[
+                    i * channels : (i + 1) * channels, h * width : (h + 1) * width
+                ]
+        return carry
+
+    w_first = height // 4
+    lax.fori_loop(0, w_first, back_step, 0)
+
+    def across(t):
+        return copy(send2.at[t], recv2.at[t], s2.at[t], r2.at[t], in_plane(t))
+
+    def pair_sum(q, k):
+        row = ((q * depth + k) * 2 + core) * shard_rows
+        return flat[pl.ds(row, PAD_ROWS), :] + recv1[q, k].astype(f32)
+
+    def across_start(t):
+        pair(t).wait_recv()
+        q = chunk(t)
+        for k in range(depth):
+            send2[t, k] = pair_sum(q, k).astype(bf16)
+        across(t).start()
+
+    loop(1, plane, early(across_start))
+
+    lax.fori_loop(w_first, height // 2, back_step, 0)
+
+    def sums_step(r, carry):
+        shift_sum, gain_sum = carry
+        dpre = gact[r + 1] * dact_s[r]
+        gact[r + 1] = dpre
+        return shift_sum + dpre, gain_sum + dpre * normed_s[r]
+
+    shift_sum, gain_sum = lax.fori_loop(0, height, sums_step, (zero_block, zero_block))
+    mean_grad = group_mean(shift_sum * gain)
+    mean_cross = group_mean(gain_sum * gain)
+
     bias_row = as_row(jnp.sum(bias_total, axis=1, keepdims=True))
     gain_row = as_row(jnp.sum(gain_sum, axis=1, keepdims=True))
     shift_row = as_row(jnp.sum(shift_sum, axis=1, keepdims=True))
-    flat[used:flat_rows, :] = jnp.zeros((flat_rows - used, LANES), f32)
     flat[used : used + 1, :] = bias_row[:, 0:128]
     flat[used + 1 : used + 2, :] = bias_row[:, 128:256]
     flat[used + 2 : used + 3, 0:64] = bias_row[:, 256:320]
@@ -216,139 +341,26 @@
     flat[used + 6 : used + 7, :] = shift_row[:, 128:256]
     flat[used + 7 : used + 8, 0:64] = shift_row[:, 256:320]
 
-    def shard_step(q, carry):
-        own_ref[q] = flat[pl.ds((2 * q + core) * shard_rows, PAD_ROWS), :]
-        other_ref[q] = flat[pl.ds((2 * q + 1 - core) * shard_rows, PAD_ROWS), :].astype(bf16)
+    last_t = (last + plane - p) % plane
+    pair_start(last_t)
+
+    def input_step(r, carry):
+        slope = gact[r + 1] * gain
+        gin_ref[r] = (rstd * (slope - mean_grad - normed_s[r] * mean_cross)).astype(bf16)
         return carry
 
-    lax.fori_loop(0, own_ref.shape[0], shard_step, 0)
-
-
-def sample_grads(x, cot, weight, gain, shift, shards, shard_rows):
-    height, channels, width = x.shape
-    f32, bf16 = jnp.float32, jnp.bfloat16
-    wide = -(-3 * channels // 256) * 256
-    flat_rows = shards * shard_rows + PAD_ROWS
-    return pl.pallas_call(
-        functools.partial(grads_kernel, shard_rows),
-        out_shape=(
-            jax.ShapeDtypeStruct(x.shape, bf16),
-            jax.ShapeDtypeStruct((shards // 2, PAD_ROWS, LANES), f32),
-            jax.ShapeDtypeStruct((shards // 2, PAD_ROWS, LANES), bf16),
-        ),
-        scratch_shapes=[
-            pltpu.VMEM((3 * channels, height * width), bf16),
-            pltpu.VMEM((wide, height * width), bf16),
-            pltpu.VMEM((3 * channels, wide), bf16),
-            pltpu.VMEM((wide // LANES, 3 * channels, LANES), f32),
-            pltpu.VMEM((flat_rows, LANES), f32),
-            pltpu.VMEM((height, channels, width), f32),
-            pltpu.VMEM((height, channels, width), f32),
-            pltpu.VMEM((height + 2, channels, width), f32),
-        ],
-        compiler_params=pltpu.CompilerParams(vmem_limit_bytes=VMEM_LIMIT),
-    )(x, cot, weight.reshape(9, channels, channels), gain[None], shift[None])
-
-
-def update_kernel(
-    split_rows,
-    own_ref,
-    other_ref,
-    master_ref,
-    first_ref,
-    second_ref,
-    gath,
-    new_master_ref,
-    new_first_ref,
-    new_second_ref,
-    recv1,
-    send2,
-    recv2,
-    acc,
-    recv3,
-    norm_line,
-    norm_plane,
-    s1,
-    r1,
-    s2,
-    r2,
-    s3,
-    r3,
-    sl,
-    rl,
-    sp,
-    rp,
-    sa,
-    ra,
-    sb,
-    rb,
-    sc,
-    rc,
-):
-    f32, bf16 = jnp.float32, jnp.bfloat16
-    plane, depth = own_ref.shape[0], own_ref.shape[1]
-    line = 2 * depth
-    grp, dp = lax.axis_index("grp"), lax.axis_index("dp")
-    p = grp * split_rows + dp // line
-    spot = dp % line
-    z, core = spot // 2, spot % 2
-    shard_rows = master_ref.shape[0]
-
-    def device(p_, spot_):
-        return (p_ // split_rows, (p_ % split_rows) * line + spot_)
-
-    def in_plane(t):
-        return device((p + t) % plane, spot)
-
-    def in_line(t):
-        return device(p, (spot + t) % line)
-
-    def in_depth(t):
-        return device(p, ((z + t) % depth) * 2 + core)
-
-    partner = device(p, z * 2 + 1 - core)
-
-    def copy(src, dst, send, recv, target):
-        return pltpu.make_async_remote_copy(
-            src_ref=src,
-            dst_ref=dst,
-            send_sem=send,
-            recv_sem=recv,
-            device_id=target,
-            device_id_type=MESH,
-        )
-
-    def loop(lo, hi, body):
-        def step(t, carry):
-            body(t)
-            return carry
-
-        lax.fori_loop(lo, hi, step, 0)
-
-    barrier = pltpu.get_barrier_semaphore()
-    loop(1, plane, lambda t: pl.semaphore_signal(barrier, inc=1, device_id=in_plane(t), device_id_type=MESH))
-    loop(1, line, lambda t: pl.semaphore_signal(barrier, inc=1, device_id=in_line(t), device_id_type=MESH))
-    pl.semaphore_wait(barrier, plane + line - 2)
-
-    def pair(t):
-        q = (p + t) % plane
-        return copy(other_ref.at[q], recv1.at[q], s1.at[t], r1.at[t], partner)
-
-    loop(1, plane, lambda t: pair(t).start())
-    pair(0).start()
-
-    def across(t):
-        return copy(send2.at[t], recv2.at[t], s2.at[t], r2.at[t], in_plane(t))
-
-    def across_start(t):
-        pair(t).wait_recv()
-        q = (p + t) % plane
-        send2[t] = (own_ref[q] + recv1[q].astype(f32)).astype(bf16)
-        across(t).start()
-
-    loop(1, plane, across_start)
+    lax.fori_loop(0, height, input_step, 0)
+
+    gin_copy = pltpu.make_async_copy(gin_ref, gin_hbm, gin_sem)
+    gin_copy.start()
+
+    @pl.when(p != last)
+    def _():
+        across_start(last_t)
+
     pair(0).wait_recv()
-    acc[...] = own_ref[p] + recv1[p].astype(f32)
+    for k in range(depth):
+        acc[k] = pair_sum(p, k)
 
     def across_take(t):
         across(t).wait_recv()
@@ -421,12 +433,24 @@
     loop(1, plane, lambda t: gather_plane(t).start())
     gather_core(0).start()
 
+    def keep(c, t):
+        q = (p + plane - t) % plane
+        return pltpu.make_async_copy(gath.at[c, q], gath_hbm.at[c, q], out_sem.at[c, t])
+
+    keep(core, 0).start()
+
     def pass_on(t):
         gather_plane(t).wait_recv()
         gather_core(t).start()
+        keep(core, t).start()
 
     loop(1, plane, pass_on)
-    loop(0, plane, lambda t: gather_core(t).wait_recv())
+
+    def take(t):
+        gather_core(t).wait_recv()
+        keep(1 - core, t).start()
+
+    loop(0, plane, take)
 
     loop(0, plane, lambda t: pair(t).wait_send())
     loop(1, plane, lambda t: across(t).wait_send())
@@ -436,40 +460,64 @@
     loop(1, depth, lambda t: gather_depth(t).wait_send())
     loop(1, plane, lambda t: gather_plane(t).wait_send())
     loop(0, plane, lambda t: gather_core(t).wait_send())
-
-
-def reduce_and_update(own, other, master, first, second, plane, depth, split_rows):
+    gin_copy.wait()
+    loop(0, plane, lambda t: keep(core, t).wait())
+    loop(0, plane, lambda t: keep(1 - core, t).wait())
+
+
+def run_layer(x, cot, weight, gain, shift, master, first, second, plane, depth, split_rows):
     f32, bf16 = jnp.float32, jnp.bfloat16
+    height, channels, width = x.shape
     line = 2 * depth
-    own = own.reshape(plane, depth, PAD_ROWS, LANES)
-    other = other.reshape(plane, depth, PAD_ROWS, LANES)
+    wide = -(-3 * channels // 256) * 256
+    flat_rows = plane * line * master.shape[0] + PAD_ROWS
     shard = jax.ShapeDtypeStruct(master.shape, f32)
-    dma = lambda n: pltpu.SemaphoreType.DMA((n,))
+    weight = weight.reshape(9, channels, channels)
+    gathered = (2, plane, depth, PAD_ROWS, LANES)
+    part = (plane, depth, PAD_ROWS, LANES)
+    dma = lambda *n: pltpu.SemaphoreType.DMA(n)
+    vmem, anywhere = pl.BlockSpec(memory_space=pltpu.VMEM), pl.BlockSpec(memory_space=pl.ANY)
     return pl.pallas_call(
-        functools.partial(update_kernel, split_rows),
+        functools.partial(layer_kernel, split_rows, plane, depth),
         out_shape=(
-            jax.ShapeDtypeStruct((2, plane, depth, PAD_ROWS, LANES), bf16),
+            jax.ShapeDtypeStruct(x.shape, bf16),
+            jax.ShapeDtypeStruct(gathered, bf16),
             shard,
             shard,
             shard,
         ),
-        in_specs=[pl.BlockSpec(memory_space=pltpu.VMEM)] * 5,
-        out_specs=[pl.BlockSpec(memory_space=pltpu.VMEM)] * 4,
+        in_specs=[vmem, vmem, anywhere, vmem, vmem, vmem, vmem, vmem],
+        out_specs=[anywhere, anywhere, vmem, vmem, vmem],
         scratch_shapes=[
-            pltpu.VMEM((plane, depth, PAD_ROWS, LANES), bf16),
-            pltpu.VMEM((plane, depth, PAD_ROWS, LANES), bf16),
-            pltpu.VMEM((plane, depth, PAD_ROWS, LANES), bf16),
+            pltpu.VMEM(weight.shape, bf16),
+            pltpu.VMEM(x.shape, bf16),
+            pltpu.VMEM(gathered, bf16),
+            pltpu.VMEM((3 * channels, height * width), bf16),
+            pltpu.VMEM((wide, height * width), bf16),
+            pltpu.VMEM((3 * channels, wide), bf16),
+            pltpu.VMEM((wide // LANES, 3 * channels, LANES), f32),
+            pltpu.VMEM((flat_rows, LANES), f32),
+            pltpu.VMEM((height, channels, width), f32),
+            pltpu.VMEM((height, channels, width), f32),
+            pltpu.VMEM((height + 2, channels, width), f32),
+            pltpu.VMEM(part, bf16),
+            pltpu.VMEM(part, bf16),
+            pltpu.VMEM(part, bf16),
+            pltpu.VMEM(part, bf16),
             pltpu.VMEM((depth, PAD_ROWS, LANES), f32),
             pltpu.VMEM((depth, PAD_ROWS, LANES), f32),
             pltpu.VMEM((line, 8, LANES), f32),
             pltpu.VMEM((plane, 8, LANES), f32),
+            pltpu.SemaphoreType.DMA,
+            pltpu.SemaphoreType.DMA,
         ]
         + [dma(n) for n in (plane, plane, plane, plane, depth, depth, line, line)]
-        + [dma(n) for n in (plane, plane, depth, depth, plane, plane, plane, plane)],
+        + [dma(n) for n in (plane, plane, depth, depth, plane, plane, plane, plane)]
+        + [dma(2, plane)],
         compiler_params=pltpu.CompilerParams(
             collective_id=0, has_side_effects=True, vmem_limit_bytes=VMEM_LIMIT
         ),
-    )(own, other, master, first, second)
+    )(x, cot, weight, gain, shift, master, first, second)
 
 
 def unpack_kernel(shard_rows, gath, weight_ref, bias_ref, gain_ref, shift_ref, flat, rows):
@@ -546,10 +594,9 @@
     shard_rows = master.shape[0] // LANES
     x = jnp.transpose(latents[0], (0, 2, 1))
     cot = jnp.transpose(cotangent[0], (0, 2, 1))
-    grad_in, own, other = sample_grads(x, cot, weight, gain, shift, groups * owners, shard_rows)
     shaped = [a.reshape(shard_rows, LANES) for a in (master, first_moment, second_moment)]
-    gath, new_master, new_first, new_second = reduce_and_update(
-        own, other, *shaped, plane, depth, split_rows
+    grad_in, gath, new_master, new_first, new_second = run_layer(
+        x, cot, weight, gain, shift, *shaped, plane, depth, split_rows
     )
     new_weight, new_bias, new_gain, new_shift = unpack(gath, channels, shard_rows)
     return (

time: 113 us -> 96.6 us (0.85)
  Pallas kernels: 103 us -> 88.5 us
  local copies, waits for them, and re-layouts: 4.32 us -> 2.89 us
    pallas_call x2 -> x1, Pallas kernels: 97.4 us -> 82.4 us  [run_layer(): pl.pallas_call(functools.partial(layer_kernel, split_rows, plane, depth),...]
    broadcast_in_dim x2 -> x0, local copies, waits for them, and re-layouts: 2.49 us -> none  [the longest x1 1.25 us: sample_grads(): gain[None]]
    unnamed x9 -> x12, local copies, waits for them, and re-layouts: 1.83 us -> 2.89 us
where the time goes in v2:
time: 96.6 us; the launch traced here: 95.9 us
  Pallas kernels  88.5 us (92%)
  other arithmetic  3.78 us (4%)
  local copies, waits for them, and re-layouts  2.89 us (3%)
    pallas_call x1, Pallas kernels, run_layer(): pl.pallas_call(functools.partial(layer_kernel, split_rows, plane, depth),...  82.4 us
    pallas_call x1, Pallas kernels, unpack(): pl.pallas_call(functools.partial(unpack_kernel, shard_rows), out_shape=(j...  6.15 us
    pallas_call x3, other arithmetic, unpack(): pl.pallas_call(functools.partial(unpack_kernel, shard_rows), out_shape=(j...  3.78 us
    unnamed x12, local copies, waits for them, and re-layouts  2.89 us

profile of v2, /device:TPU:1, one launch (start us, length us, event | category | flops | bytes accessed | tf_op | source)
XLA Modules:
  0.0 95.9 jit_solution(16780689508341460837)
XLA Ops:
  0.6 82.4 %shard_map.143 = (bf16[16,320,128]{2,1,0:T(8,128)(2,1)}, bf16[2,16,8,32,128]{4,3,2,1,0:T(8,128)(2,1)}, f32[29,128]{1,0:T(8,128)}, f32[29,128]{1,0:T(8,128)}, f32[29,128]{1,0:T(8,128)}) custom-call(bf16[16,320,128]{2,1,0:T(8,128)(2,1)} %bitcast.19, bf16[16,320,128]{2,1,0:T(8,128)(2,1)} %bitcast.20, bf16[9,320,320]{2,1,0:T(8,128)(2,1)} %bitcast.17, ...), custom_call_target="tpu_custom_call" | custom-call | tf_op jit(solution)/shard_map/pallas_call | solution.py:480
  83.0 0.0 copy-start
  83.0 6.1 %shard_map.144 = (bf16[2880,320]{1,0:T(8,128)(2,1)}, bf16[1,320]{1,0:T(2,128)(2,1)}, bf16[1,320]{1,0:T(2,128)(2,1)}, bf16[1,320]{1,0:T(2,128)(2,1)}) custom-call(bf16[2,16,8,32,128]{4,3,2,1,0:T(8,128)(2,1)} %get-tuple-element.18.gath), custom_call_target="tpu_custom_call" | custom-call | tf_op jit(solution)/shard_map/pallas_call | solution.py:577
  89.2 1.3 %reduce = bf16[320]{0:T(512)(128)(2,1)} reduce(bf16[1,320]{1,0:T(2,128)(2,1)} %get-tuple-element.20, bf16[]{:T(256)} %constant.5), dimensions={0}, to_apply=%get-tuple-element.20.reduce_sub_computation | reduce | bytes 1282 | tf_op jit(solution)/shard_map/pallas_call | solution.py:577
  90.5 1.3 %reduce.1 = bf16[320]{0:T(512)(128)(2,1)} reduce(bf16[1,320]{1,0:T(2,128)(2,1)} %get-tuple-element.21, bf16[]{:T(256)} %constant.5), dimensions={0}, to_apply=%get-tuple-element.21.reduce_sub_computation | reduce | bytes 1282 | tf_op jit(solution)/shard_map/pallas_call | solution.py:577
  91.7 1.3 %reduce.2 = bf16[320]{0:T(512)(128)(2,1)} reduce(bf16[1,320]{1,0:T(2,128)(2,1)} %get-tuple-element.22, bf16[]{:T(256)} %constant.5), dimensions={0}, to_apply=%get-tuple-element.22.reduce_sub_computation | reduce | bytes 1282 | tf_op jit(solution)/shard_map/pallas_call | solution.py:577
  93.0 0.0 copy-done
  93.0 0.0 copy-start.3
  93.0 0.0 copy-start.2
  93.0 0.0 copy-start.1
  93.0 1.1 %copy.20 = bf16[1,16,128,320]{2,3,1,0:T(8,128)(2,1)} copy(bf16[1,16,128,320]{2,3,1,0:T(8,128)(2,1)S(1)} %bitcast.18) | data formatting | bytes 2621440
  94.0 0.0 copy-done.3
  94.0 0.6 copy.21
  94.7 0.0 copy-done.2
  94.7 0.6 copy.22
  95.3 0.0 copy-done.1
  95.3 0.6 copy.23
Async XLA Ops:
  83.0 9.9 %copy-start = (bf16[16,320,128]{2,1,0:T(8,128)(2,1)S(1)}, bf16[16,320,128]{2,1,0:T(8,128)(2,1)}, u32[]{:S(2)}) copy-start(bf16[16,320,128]{2,1,0:T(8,128)(2,1)} %get-tuple-element.17) | copy-start | bytes 3932164
  93.0 1.1 %copy-start.3 = (f32[29,128]{1,0:T(8,128)S(1)}, f32[29,128]{1,0:T(8,128)}, u32[]{:S(2)}) copy-start(f32[29,128]{1,0:T(8,128)} %get-tuple-element.23) | copy-start | bytes 44548
  93.0 1.7 %copy-start.2 = (f32[29,128]{1,0:T(8,128)S(1)}, f32[29,128]{1,0:T(8,128)}, u32[]{:S(2)}) copy-start(f32[29,128]{1,0:T(8,128)} %get-tuple-element.24) | copy-start | bytes 44548
  93.0 2.3 %copy-start.1 = (f32[29,128]{1,0:T(8,128)S(1)}, f32[29,128]{1,0:T(8,128)}, u32[]{:S(2)}) copy-start(f32[29,128]{1,0:T(8,128)} %get-tuple-element.25) | copy-start | bytes 44548

commit v3 on v2

--- a/solution.py
+++ b/solution.py
@@ -46,13 +46,16 @@
     first_ref,
     second_ref,
     gin_hbm,
-    gath_hbm,
+    wout_hbm,
+    tail_ref,
     new_master_ref,
     new_first_ref,
     new_second_ref,
     w_ref,
     gin_ref,
     gath,
+    wout,
+    rows,
     act3,
     cot3,
     wcat,
@@ -388,20 +391,20 @@
 
     loop(1, line, lambda t: line_copy(t).start())
     loop(1, line, lambda t: line_copy(t).wait_recv())
-    part = norm_line[0]
+    sumsq = norm_line[0]
     for t in range(1, line):
-        part = part + norm_line[t]
-    norm_plane[0] = part
+        sumsq = sumsq + norm_line[t]
+    norm_plane[0] = sumsq
 
     def plane_copy(t):
         return copy(norm_plane.at[0], norm_plane.at[t], sp.at[t], rp.at[t], in_plane(t))
 
     loop(1, plane, lambda t: plane_copy(t).start())
     loop(1, plane, lambda t: plane_copy(t).wait_recv())
-    part = norm_plane[0]
+    sumsq = norm_plane[0]
     for t in range(1, plane):
-        part = part + norm_plane[t]
-    norm_total = jnp.sum(jnp.sum(part, axis=1, keepdims=True), axis=0, keepdims=True)
+        sumsq = sumsq + norm_plane[t]
+    norm_total = jnp.sum(jnp.sum(sumsq, axis=1, keepdims=True), axis=0, keepdims=True)
 
     clip = jnp.minimum(1.0, clip_limit / (jnp.sqrt(norm_total) + 1e-06))
     clipped = (clip * summed)[0:shard_rows]
@@ -414,43 +417,148 @@
     new_first_ref[...] = new_first
     new_second_ref[...] = new_second
     recv3[0, 0:shard_rows] = new_master
-    gath[core, p, z] = recv3[0].astype(bf16)
+    gath[core, p // gath.shape[2], p % gath.shape[2], z] = recv3[0].astype(bf16)
+
+    x_size, w_size = gath.shape[1], gath.shape[2]
+    half_depth = depth // 2
+    xi, wi = p // w_size, p % w_size
 
     def gather_depth(t):
-        mine = gath.at[core, p, z]
+        mine = gath.at[core, xi, wi, z]
         return copy(mine, mine, sa.at[t], ra.at[t], in_depth(t))
 
-    def gather_plane(t):
-        mine = gath.at[core, p]
-        return copy(mine, mine, sb.at[t], rb.at[t], in_plane(t))
-
-    def gather_core(t):
-        block = gath.at[core, (p + plane - t) % plane]
-        return copy(block, block, sc.at[t], rc.at[t], partner)
+    def back_x(t):
+        return (xi + x_size - t) % x_size
+
+    def back_w(t):
+        return (wi + w_size - t) % w_size
+
+    def part(c, h, tx, tw):
+        return gath.at[c, back_x(tx), back_w(tw), pl.ds(h * half_depth, half_depth)]
+
+    def slots_x(h, t, tw):
+        spots = (h, t, 0) if h == 0 else (h, tw, t)
+        return sb.at[spots], rb.at[spots]
+
+    def slots_w(h, t, tx):
+        spots = (h, t, 0) if h == 1 else (h, tx, t)
+        return sb.at[spots], rb.at[spots]
+
+    def along_x(h, t, tw):
+        block = part(core, h, 0, tw)
+        target = device(((xi + t) % x_size) * w_size + wi, spot)
+        return copy(block, block, *slots_x(h, t, tw), target)
+
+    def along_w(h, t, tx):
+        block = part(core, h, tx, 0)
+        target = device(xi * w_size + (wi + t) % w_size, spot)
+        return copy(block, block, *slots_w(h, t, tx), target)
+
+    def got_x(h, t, tw):
+        block = part(core, h, t, tw)
+        target = device(((xi + t) % x_size) * w_size + wi, spot)
+        return copy(block, block, *slots_x(h, t, tw), target)
+
+    def got_w(h, t, tx):
+        block = part(core, h, tx, t)
+        target = device(xi * w_size + (wi + t) % w_size, spot)
+        return copy(block, block, *slots_w(h, t, tx), target)
+
+    def gather_core(h, tx, tw):
+        block = part(core, h, tx, tw)
+        return copy(block, block, sc.at[h, tx, tw], rc.at[h, tx, tw], partner)
+
+    def got_core(h, tx, tw):
+        block = part(1 - core, h, tx, tw)
+        return copy(block, block, sc.at[h, tx, tw], rc.at[h, tx, tw], partner)
+
+    def to_flat(c, h, tx, tw):
+        sx, sw = back_x(tx), back_w(tw)
+        for k in range(half_depth):
+            spot_k = (h * half_depth + k) * 2 + c
+            row = ((sx * w_size + sw) * line + spot_k) * shard_rows
+            block = gath[c, sx, sw, h * half_depth + k].astype(f32)
+            flat[pl.ds(row, shard_rows), :] = block[0:shard_rows]
 
     loop(1, depth, lambda t: gather_depth(t).start())
     loop(1, depth, lambda t: gather_depth(t).wait_recv())
-    loop(1, plane, lambda t: gather_plane(t).start())
-    gather_core(0).start()
-
-    def keep(c, t):
-        q = (p + plane - t) % plane
-        return pltpu.make_async_copy(gath.at[c, q], gath_hbm.at[c, q], out_sem.at[c, t])
-
-    keep(core, 0).start()
-
-    def pass_on(t):
-        gather_plane(t).wait_recv()
-        gather_core(t).start()
-        keep(core, t).start()
-
-    loop(1, plane, pass_on)
-
-    def take(t):
-        gather_core(t).wait_recv()
-        keep(1 - core, t).start()
-
-    loop(0, plane, take)
+    loop(1, x_size, lambda t: along_x(0, t, 0).start())
+    loop(1, w_size, lambda t: along_w(1, t, 0).start())
+    loop(1, w_size, lambda t: along_w(0, t, 0).start())
+    loop(1, x_size, lambda t: along_x(1, t, 0).start())
+    gather_core(0, 0, 0).start()
+    gather_core(1, 0, 0).start()
+    to_flat(core, 0, 0, 0)
+    to_flat(core, 1, 0, 0)
+
+    def first_x(t):
+        got_x(0, t, 0).wait_recv()
+        loop(1, w_size, lambda s: along_w(0, s, t).start())
+        gather_core(0, t, 0).start()
+
+    def first_w(t):
+        got_w(1, t, 0).wait_recv()
+        loop(1, x_size, lambda s: along_x(1, s, t).start())
+        gather_core(1, 0, t).start()
+
+    def first(t):
+        first_x(t)
+        first_w(t)
+
+    loop(1, x_size, first)
+
+    def first_flat(t):
+        to_flat(core, 0, t, 0)
+        to_flat(core, 1, 0, t)
+
+    loop(1, x_size, first_flat)
+
+    def second(n):
+        a, b = n // (w_size - 1), n % (w_size - 1) + 1
+        got_w(0, b, a).wait_recv()
+        gather_core(0, a, b).start()
+        got_x(1, b, a).wait_recv()
+        gather_core(1, b, a).start()
+        to_flat(core, 0, a, b)
+        to_flat(core, 1, b, a)
+
+    loop(0, x_size * (w_size - 1), second)
+
+    def third(n):
+        a, b = n // w_size, n % w_size
+        got_core(0, a, b).wait_recv()
+        to_flat(1 - core, 0, a, b)
+        got_core(1, b, a).wait_recv()
+        to_flat(1 - core, 1, b, a)
+
+    loop(0, x_size * w_size, third)
+
+    five = channels * channels // LANES
+
+    def wout_copy(n):
+        place = pl.ds(pl.multiple_of(n * channels, channels), channels)
+        return pltpu.make_async_copy(wout.at[place], wout_hbm.at[place], out_sem.at[n])
+
+    def rows_step(n):
+        piece = [flat[pl.ds(n * five + b, half, stride=5), :] for b in range(5)]
+        turned = [swap_halves(piece[b]) for b in range(2, 5)]
+        even = [piece[0], piece[1], piece[2]]
+        odd = [
+            jnp.where(low, turned[0], turned[1]),
+            jnp.where(low, turned[1], turned[2]),
+            turned[2],
+        ]
+        for b in range(3):
+            rows[b, pl.ds(0, half, stride=2), :] = even[b]
+            rows[b, pl.ds(1, half, stride=2), :] = odd[b]
+        place = pl.ds(pl.multiple_of(n * channels, channels), channels)
+        wout[place, 0:128] = rows[0].astype(bf16)
+        wout[place, 128:256] = rows[1].astype(bf16)
+        wout[place, 256:channels] = rows[2, :, 0 : channels - 256].astype(bf16)
+        wout_copy(n).start()
+
+    loop(0, 9, rows_step)
+    tail_ref[...] = flat[used : used + 8, :]
 
     loop(0, plane, lambda t: pair(t).wait_send())
     loop(1, plane, lambda t: across(t).wait_send())
@@ -458,11 +566,22 @@
     loop(1, line, lambda t: line_copy(t).wait_send())
     loop(1, plane, lambda t: plane_copy(t).wait_send())
     loop(1, depth, lambda t: gather_depth(t).wait_send())
-    loop(1, plane, lambda t: gather_plane(t).wait_send())
-    loop(0, plane, lambda t: gather_core(t).wait_send())
+
+    def all_sent(n):
+        a, b = n // w_size, n % w_size
+        gather_core(0, a, b).wait_send()
+        gather_core(1, a, b).wait_send()
+
+        @pl.when(b > 0)
+        def _():
+            along_w(0, b, a).wait_send()
+            along_x(1, b, a).wait_send()
+
+    loop(0, x_size * w_size, all_sent)
+    loop(1, x_size, lambda t: along_x(0, t, 0).wait_send())
+    loop(1, w_size, lambda t: along_w(1, t, 0).wait_send())
     gin_copy.wait()
-    loop(0, plane, lambda t: keep(core, t).wait())
-    loop(0, plane, lambda t: keep(1 - core, t).wait())
+    loop(0, 9, lambda n: wout_copy(n).wait())
 
 
 def run_layer(x, cot, weight, gain, shift, master, first, second, plane, depth, split_rows):
@@ -473,7 +592,9 @@
     flat_rows = plane * line * master.shape[0] + PAD_ROWS
     shard = jax.ShapeDtypeStruct(master.shape, f32)
     weight = weight.reshape(9, channels, channels)
-    gathered = (2, plane, depth, PAD_ROWS, LANES)
+    ring_w = 2 * split_rows
+    ring_x = plane // ring_w
+    gathered = (2, ring_x, ring_w, depth, PAD_ROWS, LANES)
     part = (plane, depth, PAD_ROWS, LANES)
     dma = lambda *n: pltpu.SemaphoreType.DMA(n)
     vmem, anywhere = pl.BlockSpec(memory_space=pltpu.VMEM), pl.BlockSpec(memory_space=pl.ANY)
@@ -481,17 +602,20 @@
         functools.partial(layer_kernel, split_rows, plane, depth),
         out_shape=(
             jax.ShapeDtypeStruct(x.shape, bf16),
-            jax.ShapeDtypeStruct(gathered, bf16),
+            jax.ShapeDtypeStruct((9 * channels, channels), bf16),
+            jax.ShapeDtypeStruct((8, LANES), f32),
             shard,
             shard,
             shard,
         ),
         in_specs=[vmem, vmem, anywhere, vmem, vmem, vmem, vmem, vmem],
-        out_specs=[anywhere, anywhere, vmem, vmem, vmem],
+        out_specs=[anywhere, anywhere, vmem, vmem, vmem, vmem],
         scratch_shapes=[
             pltpu.VMEM(weight.shape, bf16),
             pltpu.VMEM(x.shape, bf16),
             pltpu.VMEM(gathered, bf16),
+            pltpu.VMEM((9 * channels, channels), bf16),
+            pltpu.VMEM((3, channels, LANES), f32),
             pltpu.VMEM((3 * channels, height * width), bf16),
             pltpu.VMEM((wide, height * width), bf16),
             pltpu.VMEM((3 * channels, wide), bf16),
@@ -512,77 +636,62 @@
             pltpu.SemaphoreType.DMA,
         ]
         + [dma(n) for n in (plane, plane, plane, plane, depth, depth, line, line)]
-        + [dma(n) for n in (plane, plane, depth, depth, plane, plane, plane, plane)]
-        + [dma(2, plane)],
+        + [dma(n) for n in (plane, plane, depth, depth)]
+        + [dma(2, ring_x, ring_w)] * 4
+        + [dma(9)],
         compiler_params=pltpu.CompilerParams(
             collective_id=0, has_side_effects=True, vmem_limit_bytes=VMEM_LIMIT
         ),
     )(x, cot, weight, gain, shift, master, first, second)
 
 
-def unpack_kernel(shard_rows, gath, weight_ref, bias_ref, gain_ref, shift_ref, flat, rows):
-    f32, bf16 = jnp.float32, jnp.bfloat16
-    plane, depth = gath.shape[1], gath.shape[2]
-    total, channels = weight_ref.shape
-
-    def shard_step(q, carry):
-        for core in range(2):
-            block = gath[core, q // depth, q % depth].astype(f32)
-            flat[pl.ds((2 * q + core) * shard_rows, PAD_ROWS), :] = block
-        return carry
-
-    lax.fori_loop(0, plane * depth, shard_step, 0)
-
-    half = channels // 2
-    low = lower_half((half, LANES))
-    five = channels * channels // LANES
-
-    def rows_step(n, carry):
-        piece = [flat[pl.ds(n * five + b, half, stride=5), :] for b in range(5)]
-        turned = [swap_halves(piece[b]) for b in range(2, 5)]
-        even = [piece[0], piece[1], piece[2]]
-        odd = [
-            jnp.where(low, turned[0], turned[1]),
-            jnp.where(low, turned[1], turned[2]),
-            turned[2],
-        ]
-        for b in range(3):
-            rows[b, pl.ds(0, half, stride=2), :] = even[b]
-            rows[b, pl.ds(1, half, stride=2), :] = odd[b]
-        place = pl.ds(pl.multiple_of(n * channels, channels), channels)
-        weight_ref[place, 0:128] = rows[0].astype(bf16)
-        weight_ref[place, 128:256] = rows[1].astype(bf16)
-        weight_ref[place, 256:channels] = rows[2, :, 0 : channels - 256].astype(bf16)
-        return carry
-
-    lax.fori_loop(0, total // channels, rows_step, 0)
-
-    used = total * channels // LANES
-    tail = [flat[used + b : used + b + 1, :].astype(bf16) for b in range(8)]
-    bias_ref[:, 0:128] = tail[0]
-    bias_ref[:, 128:256] = tail[1]
-    bias_ref[:, 256:320] = tail[2][:, 0:64]
-    gain_ref[:, 0:64] = tail[2][:, 64:128]
-    gain_ref[:, 64:192] = tail[3]
-    gain_ref[:, 192:320] = tail[4]
-    shift_ref[:, 0:128] = tail[5]
-    shift_ref[:, 128:256] = tail[6]
-    shift_ref[:, 256:320] = tail[7][:, 0:64]
-
-
-def unpack(gath, channels, shard_rows):
-    bf16, f32 = jnp.bfloat16, jnp.float32
-    shards = 2 * gath.shape[1] * gath.shape[2]
-    row = jax.ShapeDtypeStruct((1, channels), bf16)
+def finish_kernel(tail_ref, *refs):
+    bf16 = jnp.bfloat16
+    count = 5
+    sources, targets = refs[:count], refs[count : 2 * count]
+    bias_ref, gain_ref, shift_ref = refs[2 * count : 2 * count + 3]
+    stages, in_sem, out_sem = refs[2 * count + 3 : 3 * count + 3], refs[-2], refs[-1]
+    ins, outs = [], []
+    for n in range(count):
+        rows = sources[n].shape[0]
+        cuts = 4 if n < 2 else 1
+        for c in range(cuts):
+            place = pl.ds(c * (rows // cuts), rows // cuts)
+            k = len(ins)
+            ins.append(
+                pltpu.make_async_copy(sources[n].at[place], stages[n].at[place], in_sem.at[k])
+            )
+            outs.append(
+                pltpu.make_async_copy(stages[n].at[place], targets[n].at[place], out_sem.at[k])
+            )
+    for each in ins:
+        each.start()
+    tail = [tail_ref[b : b + 1, :] for b in range(8)]
+    rows = (
+        [tail[0], tail[1], tail[2][:, 0:64]],
+        [tail[2][:, 64:128], tail[3], tail[4]],
+        [tail[5], tail[6], tail[7][:, 0:64]],
+    )
+    for ref, row in zip((bias_ref, gain_ref, shift_ref), rows):
+        ref[...] = jnp.concatenate(row, axis=1).astype(bf16).reshape(ref.shape)
+    for arrived, leaving in zip(ins, outs):
+        arrived.wait()
+        leaving.start()
+    for each in outs:
+        each.wait()
+
+
+def finish(tail, results, channels):
+    row = jax.ShapeDtypeStruct((channels,), jnp.bfloat16)
+    vmem, anywhere = pl.BlockSpec(memory_space=pltpu.VMEM), pl.BlockSpec(memory_space=pl.ANY)
     return pl.pallas_call(
-        functools.partial(unpack_kernel, shard_rows),
-        out_shape=(jax.ShapeDtypeStruct((9 * channels, channels), bf16), row, row, row),
-        scratch_shapes=[
-            pltpu.VMEM((shards * shard_rows + PAD_ROWS, LANES), f32),
-            pltpu.VMEM((3, channels, LANES), f32),
-        ],
-        compiler_params=pltpu.CompilerParams(vmem_limit_bytes=VMEM_LIMIT),
-    )(gath)
+        finish_kernel,
+        out_shape=tuple(jax.ShapeDtypeStruct(r.shape, r.dtype) for r in results) + (row,) * 3,
+        in_specs=[vmem] + [anywhere] * 5,
+        out_specs=[anywhere] * 5 + [vmem] * 3,
+        scratch_shapes=[pltpu.VMEM(r.shape, r.dtype) for r in results]
+        + [pltpu.SemaphoreType.DMA((11,))] * 2,
+    )(tail, *results)
 
 
 def on_device(latents, cotangent, weight, gain, shift, master, first_moment, second_moment):
@@ -595,16 +704,18 @@
     x = jnp.transpose(latents[0], (0, 2, 1))
     cot = jnp.transpose(cotangent[0], (0, 2, 1))
     shaped = [a.reshape(shard_rows, LANES) for a in (master, first_moment, second_moment)]
-    grad_in, gath, new_master, new_first, new_second = run_layer(
+    grad_in, new_weight, tail, *state = run_layer(
         x, cot, weight, gain, shift, *shaped, plane, depth, split_rows
     )
-    new_weight, new_bias, new_gain, new_shift = unpack(gath, channels, shard_rows)
+    results = finish(tail, (grad_in, new_weight, *state), channels)
+    grad_in, new_weight, new_master, new_first, new_second = results[:5]
+    new_bias, new_gain, new_shift = results[5:]
     return (
         jnp.transpose(grad_in, (0, 2, 1))[None],
         new_weight.reshape(weight.shape),
-        new_bias.reshape(channels),
-        new_gain.reshape(channels),
-        new_shift.reshape(channels),
+        new_bias,
+        new_gain,
+        new_shift,
         new_master.reshape(-1),
         new_first.reshape(-1),
         new_second.reshape(-1),

time: 96.6 us -> 86.4 us (0.89)
  other arithmetic: 3.78 us -> 0 us
  Pallas kernels: 88.5 us -> 85.6 us
  local copies, waits for them, and re-layouts: 2.89 us -> 0 us
    pallas_call x3 -> x0, other arithmetic: 3.78 us -> none  [unpack(): pl.pallas_call(functools.partial(unpack_kernel, shard_rows), out_shape=(j...]
    unnamed x12 -> x0, local copies, waits for them, and re-layouts: 2.89 us -> none
    pallas_call x1, Pallas kernels: 6.15 us -> 4.36 us  [finish(): pl.pallas_call(finish_kernel, out_shape=tuple((jax.ShapeDtypeStruct(r.sha...]
    pallas_call x1, Pallas kernels: 82.4 us -> 81.2 us  [run_layer(): pl.pallas_call(functools.partial(layer_kernel, split_rows, plane, depth),...]
where the time goes in v3:
time: 86.4 us; the launch traced here: 86.2 us
  Pallas kernels  85.6 us (99%)
    pallas_call x1, Pallas kernels, run_layer(): pl.pallas_call(functools.partial(layer_kernel, split_rows, plane, depth),...  81.2 us
    pallas_call x1, Pallas kernels, finish(): pl.pallas_call(finish_kernel, out_shape=tuple((jax.ShapeDtypeStruct(r.sha...  4.36 us

profile of v3, /device:TPU:1, one launch (start us, length us, event | category | flops | bytes accessed | tf_op | source)
XLA Modules:
  0.0 86.2 jit_solution(15819768269458950631)
XLA Ops:
  0.6 81.2 %shard_map.143 = (bf16[16,320,128]{2,1,0:T(8,128)(2,1)}, bf16[2880,320]{1,0:T(8,128)(2,1)}, f32[8,128]{1,0:T(8,128)}, f32[29,128]{1,0:T(8,128)}, f32[29,128]{1,0:T(8,128)}, /*index=5*/f32[29,128]{1,0:T(8,128)}) custom-call(bf16[16,320,128]{2,1,0:T(8,128)(2,1)} %bitcast.18, bf16[16,320,128]{2,1,0:T(8,128)(2,1)} %bitcast.19, bf16[9,320,320]{2,1,0:T(8,128)(2,1)} %bitcast.17, ...), custom_call_target="tpu_custom_call" | custom-call | tf_op jit(solution)/shard_map/pallas_call | solution.py:601
  81.8 4.4 %shard_map.144 = (bf16[16,320,128]{2,1,0:T(8,128)(2,1)}, bf16[2880,320]{1,0:T(8,128)(2,1)}, f32[29,128]{1,0:T(8,128)}, f32[29,128]{1,0:T(8,128)}, f32[29,128]{1,...) custom-call(f32[8,128]{1,0:T(8,128)} %get-tuple-element.22.tail_ref, ...), custom_call_target="tpu_custom_call" | custom-call | tf_op jit(solution)/shard_map/pallas_call | solution.py:687

commit v4 on v3

--- a/solution.py
+++ b/solution.py
@@ -22,7 +22,7 @@
 correct_second = 0.6323045752290363
 
 MESH = pl.DeviceIdType.MESH
-VMEM_LIMIT = 60 * 1024 * 1024
+VMEM_LIMIT = 48 * 1024 * 1024
 
 
 def swap_halves(block):
@@ -37,24 +37,26 @@
     split_rows,
     plane,
     depth,
-    x_ref,
-    cot_ref,
+    x_hbm,
+    cot_hbm,
     w_hbm,
-    gain_ref,
-    shift_ref,
-    master_ref,
-    first_ref,
-    second_ref,
-    gin_hbm,
-    wout_hbm,
+    gain_hbm,
+    shift_hbm,
+    master_hbm,
+    first_hbm,
+    second_hbm,
+    gin_ref,
+    wout,
     tail_ref,
     new_master_ref,
     new_first_ref,
     new_second_ref,
+    x_ref,
+    cot_ref,
     w_ref,
-    gin_ref,
+    gain_ref,
+    shift_ref,
     gath,
-    wout,
     rows,
     act3,
     cot3,
@@ -70,10 +72,12 @@
     recv2,
     acc,
     recv3,
+    state,
+    gsum,
     norm_line,
     norm_plane,
-    w_sem,
-    gin_sem,
+    tails,
+    in_sem,
     s1,
     r1,
     s2,
@@ -84,13 +88,16 @@
     rl,
     sp,
     rp,
-    sa,
-    ra,
+    ss,
+    rs,
+    sg,
+    rg,
     sb,
     rb,
     sc,
     rc,
-    out_sem,
+    st,
+    rt,
 ):
     f32, bf16 = jnp.float32, jnp.bfloat16
     line = 2 * depth
@@ -98,7 +105,7 @@
     p = grp * split_rows + dp // line
     spot = dp % line
     z, core = spot // 2, spot % 2
-    shard_rows = master_ref.shape[0]
+    shard_rows = master_hbm.shape[0]
 
     def device(p_, spot_):
         return (p_ // split_rows, (p_ % split_rows) * line + spot_)
@@ -131,6 +138,18 @@
 
         lax.fori_loop(lo, hi, step, 0)
 
+    state[z] = jnp.zeros(state.shape[1:], f32)
+    pairs = [(x_hbm, x_ref), (gain_hbm, gain_ref), (shift_hbm, shift_ref)]
+    pairs += [(cot_hbm, cot_ref), (w_hbm, w_ref)]
+    for n, ref in enumerate((master_hbm, first_hbm, second_hbm)):
+        pairs.append((ref, state.at[z, n, pl.ds(0, shard_rows)]))
+    loads = [
+        pltpu.make_async_copy(source, target, in_sem.at[n])
+        for n, (source, target) in enumerate(pairs)
+    ]
+    for load in loads:
+        load.start()
+
     barrier = pltpu.get_barrier_semaphore()
 
     def greet(target):
@@ -138,8 +157,6 @@
 
     loop(1, plane, lambda t: greet(in_plane(t)))
     loop(1, line, lambda t: greet(in_line(t)))
-    w_copy = pltpu.make_async_copy(w_hbm, w_ref, w_sem)
-    w_copy.start()
 
     height, channels, width = x_ref.shape
     count = height * width * (channels // GROUPS)
@@ -164,6 +181,8 @@
     def as_row(column):
         return jnp.sum(eye * column, axis=0, keepdims=True)
 
+    for load in loads[:3]:
+        load.wait()
     gain = as_column(gain_ref[...].reshape(1, channels))
     shift = as_column(shift_ref[...].reshape(1, channels))
 
@@ -186,6 +205,7 @@
     act3[2 * channels : 3 * channels, (height - 1) * width : height * width] = zero_bf
     cot3[3 * channels :, :] = jnp.zeros((cot3.shape[0] - 3 * channels, cot3.shape[1]), bf16)
 
+    loads[3].wait()
     bias_total = zero_block
     for r in range(height):
         normed = (x_ref[r].astype(f32) - centre) * rstd
@@ -253,7 +273,16 @@
 
     used = 9 * channels * channels // LANES
     flat[used:flat_rows, :] = jnp.zeros((flat_rows - used, LANES), f32)
-    last = used // (shard_rows * line)
+
+    pl.semaphore_wait(barrier, plane + line - 2)
+
+    for load in loads[5:]:
+        load.wait()
+
+    def spread_state(t):
+        return copy(state.at[z], state.at[z], ss.at[t], rs.at[t], in_depth(t))
+
+    loop(1, depth, lambda t: spread_state(t).start())
 
     def chunk(t):
         return (p + t) % plane
@@ -269,19 +298,10 @@
             send1[q, k] = flat[pl.ds(row, PAD_ROWS), :].astype(bf16)
         pair(t).start()
 
-    def early(body):
-        def step(t):
-            @pl.when(chunk(t) != last)
-            def _():
-                body(t)
-
-        return step
-
-    pl.semaphore_wait(barrier, plane + line - 2)
-    loop(1, plane, early(pair_start))
-    early(pair_start)(0)
-
-    w_copy.wait()
+    loop(1, plane, pair_start)
+    pair_start(0)
+
+    loads[4].wait()
     wcat[...] = jnp.zeros_like(wcat)
     for i in range(3):
         for j in range(3):
@@ -289,6 +309,22 @@
                 3 * i + j
             ]
     gact[...] = jnp.zeros_like(gact)
+
+    def across(t):
+        return copy(send2.at[t], recv2.at[t], s2.at[t], r2.at[t], in_plane(t))
+
+    def pair_sum(q, k):
+        row = ((q * depth + k) * 2 + core) * shard_rows
+        return flat[pl.ds(row, PAD_ROWS), :] + recv1[q, k].astype(f32)
+
+    def across_start(t):
+        pair(t).wait_recv()
+        q = chunk(t)
+        for k in range(depth):
+            send2[t, k] = pair_sum(q, k).astype(bf16)
+        across(t).start()
+
+    loop(1, plane, across_start)
 
     def back_step(n, carry):
         start = pl.multiple_of(n * 256, 256)
@@ -300,26 +336,7 @@
                 ]
         return carry
 
-    w_first = height // 4
-    lax.fori_loop(0, w_first, back_step, 0)
-
-    def across(t):
-        return copy(send2.at[t], recv2.at[t], s2.at[t], r2.at[t], in_plane(t))
-
-    def pair_sum(q, k):
-        row = ((q * depth + k) * 2 + core) * shard_rows
-        return flat[pl.ds(row, PAD_ROWS), :] + recv1[q, k].astype(f32)
-
-    def across_start(t):
-        pair(t).wait_recv()
-        q = chunk(t)
-        for k in range(depth):
-            send2[t, k] = pair_sum(q, k).astype(bf16)
-        across(t).start()
-
-    loop(1, plane, early(across_start))
-
-    lax.fori_loop(w_first, height // 2, back_step, 0)
+    lax.fori_loop(0, height // 2, back_step, 0)
 
     def sums_step(r, carry):
         shift_sum, gain_sum = carry
@@ -334,18 +351,43 @@
     bias_row = as_row(jnp.sum(bias_total, axis=1, keepdims=True))
     gain_row = as_row(jnp.sum(gain_sum, axis=1, keepdims=True))
     shift_row = as_row(jnp.sum(shift_sum, axis=1, keepdims=True))
-    flat[used : used + 1, :] = bias_row[:, 0:128]
-    flat[used + 1 : used + 2, :] = bias_row[:, 128:256]
-    flat[used + 2 : used + 3, 0:64] = bias_row[:, 256:320]
-    flat[used + 2 : used + 3, 64:128] = gain_row[:, 0:64]
-    flat[used + 3 : used + 4, :] = gain_row[:, 64:192]
-    flat[used + 4 : used + 5, :] = gain_row[:, 192:320]
-    flat[used + 5 : used + 6, :] = shift_row[:, 0:128]
-    flat[used + 6 : used + 7, :] = shift_row[:, 128:256]
-    flat[used + 7 : used + 8, 0:64] = shift_row[:, 256:320]
-
-    last_t = (last + plane - p) % plane
-    pair_start(last_t)
+    tail_shard = used // shard_rows
+    tail_place, tail_spot = tail_shard // line, tail_shard % line
+    tail_z, tail_core = tail_spot // 2, tail_spot % 2
+    tail_row = used - tail_shard * shard_rows
+    owns_tail = core == tail_core
+    tails[0] = jnp.zeros(tails.shape[1:], f32)
+    tails[0, 0:1, :] = bias_row[:, 0:128]
+    tails[0, 1:2, :] = bias_row[:, 128:256]
+    tails[0, 2:3, 0:64] = bias_row[:, 256:320]
+    tails[0, 2:3, 64:128] = gain_row[:, 0:64]
+    tails[0, 3:4, :] = gain_row[:, 64:192]
+    tails[0, 4:5, :] = gain_row[:, 192:320]
+    tails[0, 5:6, :] = shift_row[:, 0:128]
+    tails[0, 6:7, :] = shift_row[:, 128:256]
+    tails[0, 7:8, 0:64] = shift_row[:, 256:320]
+
+    tail_pair = copy(tails.at[0], tails.at[plane + 1], st.at[0], rt.at[0], partner)
+
+    @pl.when(core != tail_core)
+    def _():
+        tail_pair.start()
+
+    def tail_across(t):
+        return copy(
+            tails.at[plane], tails.at[t], st.at[1], rt.at[t], device(tail_place, spot)
+        )
+
+    tail_t = (tail_place + plane - p) % plane
+
+    @pl.when(owns_tail)
+    def _():
+        tail_pair.wait_recv()
+        tails[plane] = tails[0] + tails[plane + 1]
+
+        @pl.when(p != tail_place)
+        def _():
+            tail_across(tail_t).start()
 
     def input_step(r, carry):
         slope = gact[r + 1] * gain
@@ -354,13 +396,6 @@
 
     lax.fori_loop(0, height, input_step, 0)
 
-    gin_copy = pltpu.make_async_copy(gin_ref, gin_hbm, gin_sem)
-    gin_copy.start()
-
-    @pl.when(p != last)
-    def _():
-        across_start(last_t)
-
     pair(0).wait_recv()
     for k in range(depth):
         acc[k] = pair_sum(p, k)
@@ -370,6 +405,17 @@
         acc[...] += recv2[t].astype(f32)
 
     loop(1, plane, across_take)
+
+    @pl.when(jnp.logical_and(owns_tail, p == tail_place))
+    def _():
+        entries = pl.ds(tail_row, 8)
+        acc[tail_z, entries] += tails[plane]
+
+        def tail_take(t):
+            tail_across(t).wait_recv()
+            acc[tail_z, entries] += tails[t]
+
+        loop(1, plane, tail_take)
 
     def along(t):
         return copy(acc.at[(z + t) % depth], recv3.at[t], s3.at[t], r3.at[t], in_depth(t))
@@ -384,48 +430,70 @@
     summed = jnp.where(live, summed, 0.0)
 
     squares = summed * summed
-    norm_line[0] = squares[0:8] + squares[8:16] + squares[16:24] + squares[24:32]
+    norm_line[spot] = squares[0:8] + squares[8:16] + squares[16:24] + squares[24:32]
+    gsum[z] = summed
 
     def line_copy(t):
-        return copy(norm_line.at[0], norm_line.at[t], sl.at[t], rl.at[t], in_line(t))
+        mine = norm_line.at[spot]
+        return copy(mine, mine, sl.at[t], rl.at[t], in_line(t))
+
+    def line_got(t):
+        theirs = norm_line.at[(spot + line - t) % line]
+        return copy(theirs, theirs, sl.at[t], rl.at[t], in_line(t))
+
+    def spread_sum(t):
+        return copy(gsum.at[z], gsum.at[z], sg.at[t], rg.at[t], in_depth(t))
+
+    def sum_got(t):
+        theirs = gsum.at[(z + depth - t) % depth]
+        return copy(theirs, theirs, sg.at[t], rg.at[t], in_depth(t))
+
+    def state_got(t):
+        theirs = state.at[(z + depth - t) % depth]
+        return copy(theirs, theirs, ss.at[t], rs.at[t], in_depth(t))
 
     loop(1, line, lambda t: line_copy(t).start())
-    loop(1, line, lambda t: line_copy(t).wait_recv())
+    loop(1, depth, lambda t: spread_sum(t).start())
+    loop(1, line, lambda t: line_got(t).wait_recv())
     sumsq = norm_line[0]
-    for t in range(1, line):
-        sumsq = sumsq + norm_line[t]
-    norm_plane[0] = sumsq
+    for n in range(1, line):
+        sumsq = sumsq + norm_line[n]
+    norm_plane[p] = sumsq
 
     def plane_copy(t):
-        return copy(norm_plane.at[0], norm_plane.at[t], sp.at[t], rp.at[t], in_plane(t))
+        mine = norm_plane.at[p]
+        return copy(mine, mine, sp.at[t], rp.at[t], in_plane(t))
+
+    def plane_got(t):
+        theirs = norm_plane.at[(p + plane - t) % plane]
+        return copy(theirs, theirs, sp.at[t], rp.at[t], in_plane(t))
 
     loop(1, plane, lambda t: plane_copy(t).start())
-    loop(1, plane, lambda t: plane_copy(t).wait_recv())
+    loop(1, depth, lambda t: state_got(t).wait_recv())
+    loop(1, depth, lambda t: sum_got(t).wait_recv())
+    loop(1, plane, lambda t: plane_got(t).wait_recv())
     sumsq = norm_plane[0]
-    for t in range(1, plane):
-        sumsq = sumsq + norm_plane[t]
+    for n in range(1, plane):
+        sumsq = sumsq + norm_plane[n]
     norm_total = jnp.sum(jnp.sum(sumsq, axis=1, keepdims=True), axis=0, keepdims=True)
-
     clip = jnp.minimum(1.0, clip_limit / (jnp.sqrt(norm_total) + 1e-06))
-    clipped = (clip * summed)[0:shard_rows]
-    new_first = beta_first * first_ref[...] + (1.0 - beta_first) * clipped
-    new_second = beta_second * second_ref[...] + (1.0 - beta_second) * clipped * clipped
-    step_dir = new_first / correct_first / (jnp.sqrt(new_second / correct_second) + adam_epsilon)
-    master = master_ref[...]
-    new_master = master - learn_rate * (step_dir + weight_decay * master)
-    new_master_ref[...] = new_master
-    new_first_ref[...] = new_first
-    new_second_ref[...] = new_second
-    recv3[0, 0:shard_rows] = new_master
-    gath[core, p // gath.shape[2], p % gath.shape[2], z] = recv3[0].astype(bf16)
+
+    def adam(total, master, first, second):
+        clipped = clip * total
+        new_first = beta_first * first + (1.0 - beta_first) * clipped
+        new_second = beta_second * second + (1.0 - beta_second) * clipped * clipped
+        step_dir = new_first / correct_first / (
+            jnp.sqrt(new_second / correct_second) + adam_epsilon
+        )
+        return master - learn_rate * (step_dir + weight_decay * master), new_first, new_second
 
     x_size, w_size = gath.shape[1], gath.shape[2]
+    xi, wi = p // w_size, p % w_size
+    for k in range(depth):
+        updated, _, _ = adam(gsum[k], state[k, 0], state[k, 1], state[k, 2])
+        gath[core, xi, wi, k] = updated.astype(bf16)
+
     half_depth = depth // 2
-    xi, wi = p // w_size, p % w_size
-
-    def gather_depth(t):
-        mine = gath.at[core, xi, wi, z]
-        return copy(mine, mine, sa.at[t], ra.at[t], in_depth(t))
 
     def back_x(t):
         return (xi + x_size - t) % x_size
@@ -480,8 +548,6 @@
             block = gath[c, sx, sw, h * half_depth + k].astype(f32)
             flat[pl.ds(row, shard_rows), :] = block[0:shard_rows]
 
-    loop(1, depth, lambda t: gather_depth(t).start())
-    loop(1, depth, lambda t: gather_depth(t).wait_recv())
     loop(1, x_size, lambda t: along_x(0, t, 0).start())
     loop(1, w_size, lambda t: along_w(1, t, 0).start())
     loop(1, w_size, lambda t: along_w(0, t, 0).start())
@@ -490,6 +556,9 @@
     gather_core(1, 0, 0).start()
     to_flat(core, 0, 0, 0)
     to_flat(core, 1, 0, 0)
+    results = adam(gsum[z], state[z, 0], state[z, 1], state[z, 2])
+    for ref, value in zip((new_master_ref, new_first_ref, new_second_ref), results):
+        ref[...] = value[0:shard_rows]
 
     def first_x(t):
         got_x(0, t, 0).wait_recv()
@@ -534,10 +603,6 @@
     loop(0, x_size * w_size, third)
 
     five = channels * channels // LANES
-
-    def wout_copy(n):
-        place = pl.ds(pl.multiple_of(n * channels, channels), channels)
-        return pltpu.make_async_copy(wout.at[place], wout_hbm.at[place], out_sem.at[n])
 
     def rows_step(n):
         piece = [flat[pl.ds(n * five + b, half, stride=5), :] for b in range(5)]
@@ -555,7 +620,6 @@
         wout[place, 0:128] = rows[0].astype(bf16)
         wout[place, 128:256] = rows[1].astype(bf16)
         wout[place, 256:channels] = rows[2, :, 0 : channels - 256].astype(bf16)
-        wout_copy(n).start()
 
     loop(0, 9, rows_step)
     tail_ref[...] = flat[used : used + 8, :]
@@ -565,7 +629,16 @@
     loop(1, depth, lambda t: along(t).wait_send())
     loop(1, line, lambda t: line_copy(t).wait_send())
     loop(1, plane, lambda t: plane_copy(t).wait_send())
-    loop(1, depth, lambda t: gather_depth(t).wait_send())
+    loop(1, depth, lambda t: spread_state(t).wait_send())
+    loop(1, depth, lambda t: spread_sum(t).wait_send())
+
+    @pl.when(core != tail_core)
+    def _():
+        tail_pair.wait_send()
+
+    @pl.when(jnp.logical_and(owns_tail, p != tail_place))
+    def _():
+        tail_across(tail_t).wait_send()
 
     def all_sent(n):
         a, b = n // w_size, n % w_size
@@ -580,8 +653,6 @@
     loop(0, x_size * w_size, all_sent)
     loop(1, x_size, lambda t: along_x(0, t, 0).wait_send())
     loop(1, w_size, lambda t: along_w(1, t, 0).wait_send())
-    gin_copy.wait()
-    loop(0, 9, lambda n: wout_copy(n).wait())
 
 
 def run_layer(x, cot, weight, gain, shift, master, first, second, plane, depth, split_rows):
@@ -590,31 +661,35 @@
     line = 2 * depth
     wide = -(-3 * channels // 256) * 256
     flat_rows = plane * line * master.shape[0] + PAD_ROWS
-    shard = jax.ShapeDtypeStruct(master.shape, f32)
+    shard = pltpu.VMEM(master.shape, f32)
     weight = weight.reshape(9, channels, channels)
     ring_w = 2 * split_rows
     ring_x = plane // ring_w
     gathered = (2, ring_x, ring_w, depth, PAD_ROWS, LANES)
     part = (plane, depth, PAD_ROWS, LANES)
     dma = lambda *n: pltpu.SemaphoreType.DMA(n)
-    vmem, anywhere = pl.BlockSpec(memory_space=pltpu.VMEM), pl.BlockSpec(memory_space=pl.ANY)
+    vmem, hbm = pl.BlockSpec(memory_space=pltpu.VMEM), pl.BlockSpec(memory_space=pltpu.HBM)
+    operands = (x, cot, weight, gain, shift, master, first, second)
+    operands = [pltpu.with_memory_space_constraint(a, pltpu.HBM) for a in operands]
     return pl.pallas_call(
         functools.partial(layer_kernel, split_rows, plane, depth),
         out_shape=(
-            jax.ShapeDtypeStruct(x.shape, bf16),
-            jax.ShapeDtypeStruct((9 * channels, channels), bf16),
-            jax.ShapeDtypeStruct((8, LANES), f32),
+            pltpu.VMEM(x.shape, bf16),
+            pltpu.VMEM((9 * channels, channels), bf16),
+            pltpu.VMEM((8, LANES), f32),
             shard,
             shard,
             shard,
         ),
-        in_specs=[vmem, vmem, anywhere, vmem, vmem, vmem, vmem, vmem],
-        out_specs=[anywhere, anywhere, vmem, vmem, vmem, vmem],
+        in_specs=[hbm] * 8,
+        out_specs=[vmem] * 6,
         scratch_shapes=[
+            pltpu.VMEM(x.shape, bf16),
+            pltpu.VMEM(x.shape, bf16),
             pltpu.VMEM(weight.shape, bf16),
-            pltpu.VMEM(x.shape, bf16),
+            pltpu.VMEM(gain.shape, f32),
+            pltpu.VMEM(shift.shape, f32),
             pltpu.VMEM(gathered, bf16),
-            pltpu.VMEM((9 * channels, channels), bf16),
             pltpu.VMEM((3, channels, LANES), f32),
             pltpu.VMEM((3 * channels, height * width), bf16),
             pltpu.VMEM((wide, height * width), bf16),
@@ -630,41 +705,31 @@
             pltpu.VMEM(part, bf16),
             pltpu.VMEM((depth, PAD_ROWS, LANES), f32),
             pltpu.VMEM((depth, PAD_ROWS, LANES), f32),
+            pltpu.VMEM((depth, 3, PAD_ROWS, LANES), f32),
+            pltpu.VMEM((depth, PAD_ROWS, LANES), f32),
             pltpu.VMEM((line, 8, LANES), f32),
             pltpu.VMEM((plane, 8, LANES), f32),
-            pltpu.SemaphoreType.DMA,
-            pltpu.SemaphoreType.DMA,
+            pltpu.VMEM((plane + 2, 8, LANES), f32),
+            dma(8),
         ]
         + [dma(n) for n in (plane, plane, plane, plane, depth, depth, line, line)]
-        + [dma(n) for n in (plane, plane, depth, depth)]
+        + [dma(n) for n in (plane, plane, depth, depth, depth, depth)]
         + [dma(2, ring_x, ring_w)] * 4
-        + [dma(9)],
+        + [dma(2), dma(plane)],
         compiler_params=pltpu.CompilerParams(
             collective_id=0, has_side_effects=True, vmem_limit_bytes=VMEM_LIMIT
         ),
-    )(x, cot, weight, gain, shift, master, first, second)
+    )(*operands)
 
 
 def finish_kernel(tail_ref, *refs):
-    bf16 = jnp.bfloat16
     count = 5
     sources, targets = refs[:count], refs[count : 2 * count]
-    bias_ref, gain_ref, shift_ref = refs[2 * count : 2 * count + 3]
-    stages, in_sem, out_sem = refs[2 * count + 3 : 3 * count + 3], refs[-2], refs[-1]
-    ins, outs = [], []
-    for n in range(count):
-        rows = sources[n].shape[0]
-        cuts = 4 if n < 2 else 1
-        for c in range(cuts):
-            place = pl.ds(c * (rows // cuts), rows // cuts)
-            k = len(ins)
-            ins.append(
-                pltpu.make_async_copy(sources[n].at[place], stages[n].at[place], in_sem.at[k])
-            )
-            outs.append(
-                pltpu.make_async_copy(stages[n].at[place], targets[n].at[place], out_sem.at[k])
-            )
-    for each in ins:
+    rows_out, sems = refs[2 * count : 2 * count + 3], refs[-1]
+    copies = [
+        pltpu.make_async_copy(sources[n], targets[n], sems.at[n]) for n in range(count)
+    ]
+    for each in copies:
         each.start()
     tail = [tail_ref[b : b + 1, :] for b in range(8)]
     rows = (
@@ -672,26 +737,24 @@
         [tail[2][:, 64:128], tail[3], tail[4]],
         [tail[5], tail[6], tail[7][:, 0:64]],
     )
-    for ref, row in zip((bias_ref, gain_ref, shift_ref), rows):
-        ref[...] = jnp.concatenate(row, axis=1).astype(bf16).reshape(ref.shape)
-    for arrived, leaving in zip(ins, outs):
-        arrived.wait()
-        leaving.start()
-    for each in outs:
+    for ref, row in zip(rows_out, rows):
+        ref[...] = jnp.concatenate(row, axis=1).astype(ref.dtype).reshape(ref.shape)
+    for each in copies:
         each.wait()
 
 
 def finish(tail, results, channels):
     row = jax.ShapeDtypeStruct((channels,), jnp.bfloat16)
     vmem, anywhere = pl.BlockSpec(memory_space=pltpu.VMEM), pl.BlockSpec(memory_space=pl.ANY)
+    pinned = [pltpu.with_memory_space_constraint(r, pltpu.VMEM) for r in (tail, *results)]
     return pl.pallas_call(
         finish_kernel,
         out_shape=tuple(jax.ShapeDtypeStruct(r.shape, r.dtype) for r in results) + (row,) * 3,
-        in_specs=[vmem] + [anywhere] * 5,
+        in_specs=[vmem] * 6,
         out_specs=[anywhere] * 5 + [vmem] * 3,
-        scratch_shapes=[pltpu.VMEM(r.shape, r.dtype) for r in results]
-        + [pltpu.SemaphoreType.DMA((11,))] * 2,
-    )(tail, *results)
+        scratch_shapes=[pltpu.SemaphoreType.DMA((5,))],
+        compiler_params=pltpu.CompilerParams(vmem_limit_bytes=4 * 1024 * 1024),
+    )(*pinned)
 
 
 def on_device(latents, cotangent, weight, gain, shift, master, first_moment, second_moment):

time: 86.4 us -> 73.5 us (0.85)
  Pallas kernels: 85.6 us -> 72.7 us
    pallas_call x1, Pallas kernels: 81.2 us -> 70.3 us  [run_layer(): pl.pallas_call(functools.partial(layer_kernel, split_rows, plane, depth),...]
    pallas_call x1, Pallas kernels: 4.36 us -> 2.41 us  [finish(): pl.pallas_call(finish_kernel, out_shape=tuple((jax.ShapeDtypeStruct(r.sha...]
where the time goes in v4:
time: 73.5 us; the launch traced here: 73.4 us
  Pallas kernels  72.7 us (99%)
    pallas_call x1, Pallas kernels, run_layer(): pl.pallas_call(functools.partial(layer_kernel, split_rows, plane, depth),...  70.3 us
    pallas_call x1, Pallas kernels, finish(): pl.pallas_call(finish_kernel, out_shape=tuple((jax.ShapeDtypeStruct(r.sha...  2.41 us

profile of v4, /device:TPU:1, one launch (start us, length us, event | category | flops | bytes accessed | tf_op | source)
XLA Modules:
  0.0 73.4 jit_solution(13151565167890026798)
XLA Ops:
  0.6 70.3 %shard_map.143 = (bf16[16,320,128]{2,1,0:T(8,128)(2,1)S(1)}, bf16[2880,320]{1,0:T(8,128)(2,1)S(1)}, f32[8,128]{1,0:T(8,128)S(1)}, f32[29,128]{1,0:T(8,128)S(1)},...) custom-call(bf16[16,320,128]{2,1,0:T(8,128)(2,1)} %bitcast.18, bf16[16,320,128]{2,1,0:T(8,128)(2,1)} %bitcast.19, ...), custom_call_target="tpu_custom_call" | custom-call | tf_op jit(solution)/shard_map/pallas_call | solution.py:674
  71.0 2.4 %shard_map.144 = (bf16[16,320,128]{2,1,0:T(8,128)(2,1)}, bf16[2880,320]{1,0:T(8,128)(2,1)}, f32[29,128]{1,0:T(8,128)}, f32[29,128]{1,0:T(8,128)}, f32[29,128]{1,...) custom-call(f32[8,128]{1,0:T(8,128)S(1)} %get-tuple-element.22.tail_ref, ...), custom_call_target="tpu_custom_call" | custom-call | tf_op jit(solution)/shard_map/pallas_call | solution.py:750

commit v5 on v4

--- a/solution.py
+++ b/solution.py
@@ -77,6 +77,7 @@
     norm_line,
     norm_plane,
     tails,
+    tail_line,
     in_sem,
     s1,
     r1,
@@ -227,19 +228,15 @@
         cot3[channels : 2 * channels, place] = cot_ref[r]
         cot3[2 * channels : 3 * channels, place] = behind.astype(bf16)
 
-    def kernel_step(n, carry):
-        start = pl.multiple_of(n * 256, 256)
+    for n in range(cot3.shape[0] // 256):
         block = lax.dot_general(
             act3[...],
-            cot3[pl.ds(start, 256), :],
+            cot3[n * 256 : (n + 1) * 256, :],
             (((1,), (1,)), ((), ())),
             preferred_element_type=f32,
         )
         kgrad[2 * n] = block[:, :LANES]
         kgrad[2 * n + 1] = block[:, LANES:]
-        return carry
-
-    lax.fori_loop(0, cot3.shape[0] // 256, kernel_step, 0)
 
     half = channels // 2
     low = lower_half((half, LANES))
@@ -276,16 +273,18 @@
 
     pl.semaphore_wait(barrier, plane + line - 2)
 
-    for load in loads[5:]:
-        load.wait()
-
-    def spread_state(t):
-        return copy(state.at[z], state.at[z], ss.at[t], rs.at[t], in_depth(t))
-
-    loop(1, depth, lambda t: spread_state(t).start())
+    def far_first(n):
+        return jnp.where(n == 0, 2, jnp.where(n == 1, 1, jnp.where(n == 2, 3, 0)))
+
+    x_size, w_size = gath.shape[1], gath.shape[2]
+    xi, wi = p // w_size, p % w_size
+    yi = (wi % 2) * 2 + wi // 2
+    own_t = plane - 1
 
     def chunk(t):
-        return (p + t) % plane
+        x_to = (xi + far_first(t // 4)) % x_size
+        y_to = (yi + far_first(t % 4)) % w_size
+        return x_to * w_size + (y_to % 2) * 2 + y_to // 2
 
     def pair(t):
         q = chunk(t)
@@ -298,8 +297,37 @@
             send1[q, k] = flat[pl.ds(row, PAD_ROWS), :].astype(bf16)
         pair(t).start()
 
-    loop(1, plane, pair_start)
-    pair_start(0)
+    def across(t):
+        return copy(send2.at[t], recv2.at[t], s2.at[t], r2.at[t], device(chunk(t), spot))
+
+    def pair_sum(q, k):
+        row = ((q * depth + k) * 2 + core) * shard_rows
+        return flat[pl.ds(row, PAD_ROWS), :] + recv1[q, k].astype(f32)
+
+    def across_start(t):
+        pair(t).wait_recv()
+        q = chunk(t)
+        for k in range(depth):
+            send2[t, k] = pair_sum(q, k).astype(bf16)
+        across(t).start()
+
+    lead = 3
+    loop(0, lead, pair_start)
+
+    def both(t):
+        pair_start(t + lead)
+        across_start(t)
+
+    loop(0, plane - lead, both)
+    loop(plane - lead, own_t, across_start)
+
+    for load in loads[5:]:
+        load.wait()
+
+    def spread_state(t):
+        return copy(state.at[z], state.at[z], ss.at[t], rs.at[t], in_depth(t))
+
+    loop(1, depth, lambda t: spread_state(t).start())
 
     loads[4].wait()
     wcat[...] = jnp.zeros_like(wcat)
@@ -310,33 +338,17 @@
             ]
     gact[...] = jnp.zeros_like(gact)
 
-    def across(t):
-        return copy(send2.at[t], recv2.at[t], s2.at[t], r2.at[t], in_plane(t))
-
-    def pair_sum(q, k):
-        row = ((q * depth + k) * 2 + core) * shard_rows
-        return flat[pl.ds(row, PAD_ROWS), :] + recv1[q, k].astype(f32)
-
-    def across_start(t):
-        pair(t).wait_recv()
-        q = chunk(t)
-        for k in range(depth):
-            send2[t, k] = pair_sum(q, k).astype(bf16)
-        across(t).start()
-
-    loop(1, plane, across_start)
-
     def back_step(n, carry):
-        start = pl.multiple_of(n * 256, 256)
-        block = jnp.dot(wcat[...], cot3[:, pl.ds(start, 256)], preferred_element_type=f32)
+        start = pl.multiple_of(n * 512, 512)
+        block = jnp.dot(wcat[...], cot3[:, pl.ds(start, 512)], preferred_element_type=f32)
         for i in range(3):
-            for h in range(2):
-                gact[2 * n + h + i] += block[
+            for h in range(4):
+                gact[4 * n + h + i] += block[
                     i * channels : (i + 1) * channels, h * width : (h + 1) * width
                 ]
         return carry
 
-    lax.fori_loop(0, height // 2, back_step, 0)
+    lax.fori_loop(0, height // 4, back_step, 0)
 
     def sums_step(r, carry):
         shift_sum, gain_sum = carry
@@ -396,7 +408,7 @@
 
     lax.fori_loop(0, height, input_step, 0)
 
-    pair(0).wait_recv()
+    pair(own_t).wait_recv()
     for k in range(depth):
         acc[k] = pair_sum(p, k)
 
@@ -404,25 +416,46 @@
         across(t).wait_recv()
         acc[...] += recv2[t].astype(f32)
 
-    loop(1, plane, across_take)
-
-    @pl.when(jnp.logical_and(owns_tail, p == tail_place))
+    loop(0, own_t, across_take)
+
+    def along(t):
+        return copy(acc.at[(z + t) % depth], recv3.at[t], s3.at[t], r3.at[t], in_depth(t))
+
+    loop(1, depth, lambda t: along(t).start())
+    recv3[0] = acc[z]
+    at_tail = jnp.logical_and(owns_tail, p == tail_place)
+
+    def tail_along(t):
+        return copy(tails.at[0], tail_line.at[t], st.at[2], rt.at[plane + t], device(p, tail_spot))
+
+    tail_zt = (tail_z + depth - z) % depth
+
+    @pl.when(at_tail)
+    def _():
+        def tail_take(t):
+            tail_across(t).wait_recv()
+            tails[plane] += tails[t]
+
+        loop(1, plane, tail_take)
+        tails[0] = tails[plane]
+
+        @pl.when(z != tail_z)
+        def _():
+            tail_along(tail_zt).start()
+
+    loop(1, depth, lambda t: along(t).wait_recv())
+
+    @pl.when(jnp.logical_and(at_tail, z == tail_z))
     def _():
         entries = pl.ds(tail_row, 8)
-        acc[tail_z, entries] += tails[plane]
-
-        def tail_take(t):
-            tail_across(t).wait_recv()
-            acc[tail_z, entries] += tails[t]
-
-        loop(1, plane, tail_take)
-
-    def along(t):
-        return copy(acc.at[(z + t) % depth], recv3.at[t], s3.at[t], r3.at[t], in_depth(t))
-
-    loop(1, depth, lambda t: along(t).start())
-    recv3[0] = acc[z]
-    loop(1, depth, lambda t: along(t).wait_recv())
+        recv3[0, entries] += tails[0]
+
+        def tail_sum(t):
+            tail_along(t).wait_recv()
+            recv3[0, entries] += tail_line[t]
+
+        loop(1, depth, tail_sum)
+
     summed = recv3[0]
     for t in range(1, depth):
         summed = summed + recv3[t]
@@ -487,8 +520,6 @@
         )
         return master - learn_rate * (step_dir + weight_decay * master), new_first, new_second
 
-    x_size, w_size = gath.shape[1], gath.shape[2]
-    xi, wi = p // w_size, p % w_size
     for k in range(depth):
         updated, _, _ = adam(gsum[k], state[k, 0], state[k, 1], state[k, 2])
         gath[core, xi, wi, k] = updated.astype(bf16)
@@ -625,7 +656,7 @@
     tail_ref[...] = flat[used : used + 8, :]
 
     loop(0, plane, lambda t: pair(t).wait_send())
-    loop(1, plane, lambda t: across(t).wait_send())
+    loop(0, own_t, lambda t: across(t).wait_send())
     loop(1, depth, lambda t: along(t).wait_send())
     loop(1, line, lambda t: line_copy(t).wait_send())
     loop(1, plane, lambda t: plane_copy(t).wait_send())
@@ -639,6 +670,10 @@
     @pl.when(jnp.logical_and(owns_tail, p != tail_place))
     def _():
         tail_across(tail_t).wait_send()
+
+    @pl.when(jnp.logical_and(at_tail, z != tail_z))
+    def _():
+        tail_along(tail_zt).wait_send()
 
     def all_sent(n):
         a, b = n // w_size, n % w_size
@@ -710,12 +745,13 @@
             pltpu.VMEM((line, 8, LANES), f32),
             pltpu.VMEM((plane, 8, LANES), f32),
             pltpu.VMEM((plane + 2, 8, LANES), f32),
+            pltpu.VMEM((depth, 8, LANES), f32),
             dma(8),
         ]
         + [dma(n) for n in (plane, plane, plane, plane, depth, depth, line, line)]
         + [dma(n) for n in (plane, plane, depth, depth, depth, depth)]
         + [dma(2, ring_x, ring_w)] * 4
-        + [dma(2), dma(plane)],
+        + [dma(3), dma(plane + depth)],
         compiler_params=pltpu.CompilerParams(
             collective_id=0, has_side_effects=True, vmem_limit_bytes=VMEM_LIMIT
         ),

time: 73.5 us -> 68.7 us (0.935)
  Pallas kernels: 72.7 us -> 68 us
    pallas_call x1, Pallas kernels: 70.3 us -> 65.6 us  [run_layer(): pl.pallas_call(functools.partial(layer_kernel, split_rows, plane, depth),...]
where the time goes in v5:
time: 68.7 us; the launch traced here: 68.6 us
  Pallas kernels  68 us (99%)
    pallas_call x1, Pallas kernels, run_layer(): pl.pallas_call(functools.partial(layer_kernel, split_rows, plane, depth),...  65.6 us
    pallas_call x1, Pallas kernels, finish(): pl.pallas_call(finish_kernel, out_shape=tuple((jax.ShapeDtypeStruct(r.sha...  2.41 us

profile of v5, /device:TPU:1, one launch (start us, length us, event | category | flops | bytes accessed | tf_op | source)
XLA Modules:
  0.0 68.6 jit_solution(105775091683434404)
XLA Ops:
  0.6 65.6 %shard_map.143 = (bf16[16,320,128]{2,1,0:T(8,128)(2,1)S(1)}, bf16[2880,320]{1,0:T(8,128)(2,1)S(1)}, f32[8,128]{1,0:T(8,128)S(1)}, f32[29,128]{1,0:T(8,128)S(1)},...) custom-call(bf16[16,320,128]{2,1,0:T(8,128)(2,1)} %bitcast.18, bf16[16,320,128]{2,1,0:T(8,128)(2,1)} %bitcast.19, ...), custom_call_target="tpu_custom_call" | custom-call | tf_op jit(solution)/shard_map/pallas_call | solution.py:709
  66.2 2.4 %shard_map.144 = (bf16[16,320,128]{2,1,0:T(8,128)(2,1)}, bf16[2880,320]{1,0:T(8,128)(2,1)}, f32[29,128]{1,0:T(8,128)}, f32[29,128]{1,0:T(8,128)}, f32[29,128]{1,...) custom-call(f32[8,128]{1,0:T(8,128)S(1)} %get-tuple-element.22.tail_ref, ...), custom_call_target="tpu_custom_call" | custom-call | tf_op jit(solution)/shard_map/pallas_call | solution.py:786

commit v6 on v5

--- a/solution.py
+++ b/solution.py
@@ -77,7 +77,10 @@
     norm_line,
     norm_plane,
     tails,
-    tail_line,
+    sendz,
+    recvz,
+    zacc,
+    recvf,
     in_sem,
     s1,
     r1,
@@ -99,6 +102,10 @@
     rc,
     st,
     rt,
+    sz,
+    rz,
+    sf,
+    rf,
 ):
     f32, bf16 = jnp.float32, jnp.bfloat16
     line = 2 * depth
@@ -200,10 +207,22 @@
     spread = group_mean(lax.fori_loop(0, height, spread_step, zero_block))
     rstd = lax.rsqrt(spread + norm_epsilon)
 
+    pl.semaphore_wait(barrier, plane + line - 2)
+
+    for load in loads[5:]:
+        load.wait()
+
+    def spread_state(t):
+        return copy(state.at[z], state.at[z], ss.at[t], rs.at[t], in_depth(t))
+
+    loop(1, depth, lambda t: spread_state(t).start())
+
     lane = lax.broadcasted_iota(jnp.int32, (channels, width), 1)
     zero_bf = jnp.zeros((channels, width), bf16)
     act3[0:channels, 0:width] = zero_bf
     act3[2 * channels : 3 * channels, (height - 1) * width : height * width] = zero_bf
+    cot3[:, 0:width] = jnp.zeros((cot3.shape[0], width), bf16)
+    cot3[:, (height + 1) * width :] = jnp.zeros((cot3.shape[0], width), bf16)
     cot3[3 * channels :, :] = jnp.zeros((cot3.shape[0] - 3 * channels, cot3.shape[1]), bf16)
 
     loads[3].wait()
@@ -221,7 +240,7 @@
                 act3[i * channels : (i + 1) * channels, dest * width : (dest + 1) * width] = act
         cot = cot_ref[r].astype(f32)
         bias_total = bias_total + cot
-        place = slice(r * width, (r + 1) * width)
+        place = slice((r + 1) * width, (r + 2) * width)
         ahead = jnp.where(lane < width - 1, pltpu.roll(cot, width - 1, axis=1), 0.0)
         behind = jnp.where(lane > 0, pltpu.roll(cot, 1, axis=1), 0.0)
         cot3[0:channels, place] = ahead.astype(bf16)
@@ -231,7 +250,7 @@
     for n in range(cot3.shape[0] // 256):
         block = lax.dot_general(
             act3[...],
-            cot3[n * 256 : (n + 1) * 256, :],
+            cot3[n * 256 : (n + 1) * 256, width : (height + 1) * width],
             (((1,), (1,)), ((), ())),
             preferred_element_type=f32,
         )
@@ -271,7 +290,6 @@
     used = 9 * channels * channels // LANES
     flat[used:flat_rows, :] = jnp.zeros((flat_rows - used, LANES), f32)
 
-    pl.semaphore_wait(barrier, plane + line - 2)
 
     def far_first(n):
         return jnp.where(n == 0, 2, jnp.where(n == 1, 1, jnp.where(n == 2, 3, 0)))
@@ -282,6 +300,7 @@
     own_t = plane - 1
 
     def chunk(t):
+        t = jnp.where(t == 3, 4, jnp.where(t == 4, 3, t))
         x_to = (xi + far_first(t // 4)) % x_size
         y_to = (yi + far_first(t % 4)) % w_size
         return x_to * w_size + (y_to % 2) * 2 + y_to // 2
@@ -311,23 +330,33 @@
             send2[t, k] = pair_sum(q, k).astype(bf16)
         across(t).start()
 
-    lead = 3
-    loop(0, lead, pair_start)
+    far, lead = zacc.shape[0], 4
+
+    def far_step(t):
+        pair_start(t + lead)
+        pair(t).wait_recv()
+        q = chunk(t)
+        for k in range(depth):
+            sendz[k, t] = pair_sum(q, k).astype(bf16)
+        zacc[t] = pair_sum(q, z)
+
+    def far_along(t):
+        return copy(
+            sendz.at[(z + t) % depth], recvz.at[t], sz.at[t], rz.at[t], in_depth(t)
+        )
+
+    def far_across(t):
+        return copy(zacc.at[t], recvf.at[t], sf.at[t], rf.at[t], device(chunk(t), spot))
 
     def both(t):
         pair_start(t + lead)
         across_start(t)
 
-    loop(0, plane - lead, both)
+    loop(0, lead, pair_start)
+    loop(0, far, far_step)
+    loop(1, depth, lambda t: far_along(t).start())
+    loop(far, plane - lead, both)
     loop(plane - lead, own_t, across_start)
-
-    for load in loads[5:]:
-        load.wait()
-
-    def spread_state(t):
-        return copy(state.at[z], state.at[z], ss.at[t], rs.at[t], in_depth(t))
-
-    loop(1, depth, lambda t: spread_state(t).start())
 
     loads[4].wait()
     wcat[...] = jnp.zeros_like(wcat)
@@ -336,27 +365,28 @@
             wcat[i * channels : (i + 1) * channels, j * channels : (j + 1) * channels] = w_ref[
                 3 * i + j
             ]
-    gact[...] = jnp.zeros_like(gact)
 
     def back_step(n, carry):
-        start = pl.multiple_of(n * 512, 512)
-        block = jnp.dot(wcat[...], cot3[:, pl.ds(start, 512)], preferred_element_type=f32)
+        shift_sum, gain_sum = carry
+        block = None
         for i in range(3):
-            for h in range(4):
-                gact[4 * n + h + i] += block[
-                    i * channels : (i + 1) * channels, h * width : (h + 1) * width
-                ]
-        return carry
-
-    lax.fori_loop(0, height // 4, back_step, 0)
-
-    def sums_step(r, carry):
-        shift_sum, gain_sum = carry
-        dpre = gact[r + 1] * dact_s[r]
-        gact[r + 1] = dpre
-        return shift_sum + dpre, gain_sum + dpre * normed_s[r]
-
-    shift_sum, gain_sum = lax.fori_loop(0, height, sums_step, (zero_block, zero_block))
+            start = pl.multiple_of((2 * n + 2 - i) * width, width)
+            term = jnp.dot(
+                wcat[i * channels : (i + 1) * channels, :],
+                cot3[:, pl.ds(start, 2 * width)],
+                preferred_element_type=f32,
+            )
+            block = term if block is None else block + term
+        for h in range(2):
+            dpre = block[:, h * width : (h + 1) * width] * dact_s[2 * n + h]
+            gact[2 * n + h] = dpre
+            shift_sum = shift_sum + dpre
+            gain_sum = gain_sum + dpre * normed_s[2 * n + h]
+        return shift_sum, gain_sum
+
+    shift_sum, gain_sum = lax.fori_loop(
+        0, height // 2, back_step, (zero_block, zero_block)
+    )
     mean_grad = group_mean(shift_sum * gain)
     mean_cross = group_mean(gain_sum * gain)
 
@@ -392,6 +422,13 @@
 
     tail_t = (tail_place + plane - p) % plane
 
+    def far_take(t):
+        far_along(t).wait_recv()
+        zacc[...] += recvz[t].astype(f32)
+
+    loop(1, depth, far_take)
+    loop(0, far, lambda t: far_across(t).start())
+
     @pl.when(owns_tail)
     def _():
         tail_pair.wait_recv()
@@ -401,13 +438,6 @@
         def _():
             tail_across(tail_t).start()
 
-    def input_step(r, carry):
-        slope = gact[r + 1] * gain
-        gin_ref[r] = (rstd * (slope - mean_grad - normed_s[r] * mean_cross)).astype(bf16)
-        return carry
-
-    lax.fori_loop(0, height, input_step, 0)
-
     pair(own_t).wait_recv()
     for k in range(depth):
         acc[k] = pair_sum(p, k)
@@ -416,54 +446,46 @@
         across(t).wait_recv()
         acc[...] += recv2[t].astype(f32)
 
-    loop(0, own_t, across_take)
+    loop(far, own_t, across_take)
 
     def along(t):
         return copy(acc.at[(z + t) % depth], recv3.at[t], s3.at[t], r3.at[t], in_depth(t))
 
     loop(1, depth, lambda t: along(t).start())
-    recv3[0] = acc[z]
-    at_tail = jnp.logical_and(owns_tail, p == tail_place)
-
-    def tail_along(t):
-        return copy(tails.at[0], tail_line.at[t], st.at[2], rt.at[plane + t], device(p, tail_spot))
-
-    tail_zt = (tail_z + depth - z) % depth
-
-    @pl.when(at_tail)
+    def input_step(r, carry):
+        slope = gact[r] * gain
+        gin_ref[r] = (rstd * (slope - mean_grad - normed_s[r] * mean_cross)).astype(bf16)
+        return carry
+
+    lax.fori_loop(0, height, input_step, 0)
+
+    loop(1, depth, lambda t: along(t).wait_recv())
+    summed = acc[z]
+    for t in range(1, depth):
+        summed = summed + recv3[t]
+    loop(0, far, lambda t: far_across(t).wait_recv())
+    for t in range(far):
+        summed = summed + recvf[t]
+    live = lax.broadcasted_iota(jnp.int32, summed.shape, 0) < shard_rows
+    summed = jnp.where(live, summed, 0.0)
+
+    squares = summed * summed
+    squares = jnp.sum(squares, axis=0, keepdims=True)
+    squares = squares + swap_halves(squares)
+    row8 = lax.broadcasted_iota(jnp.int32, (8, LANES), 0)
+    spare = jnp.logical_and(row8 == 7, jnp.logical_not(lower_half((8, LANES))))
+    tails[plane + 1] = jnp.where(spare, squares, 0.0)
+
+    @pl.when(jnp.logical_and(owns_tail, p == tail_place))
     def _():
         def tail_take(t):
             tail_across(t).wait_recv()
             tails[plane] += tails[t]
 
         loop(1, plane, tail_take)
-        tails[0] = tails[plane]
-
-        @pl.when(z != tail_z)
-        def _():
-            tail_along(tail_zt).start()
-
-    loop(1, depth, lambda t: along(t).wait_recv())
-
-    @pl.when(jnp.logical_and(at_tail, z == tail_z))
-    def _():
-        entries = pl.ds(tail_row, 8)
-        recv3[0, entries] += tails[0]
-
-        def tail_sum(t):
-            tail_along(t).wait_recv()
-            recv3[0, entries] += tail_line[t]
-
-        loop(1, depth, tail_sum)
-
-    summed = recv3[0]
-    for t in range(1, depth):
-        summed = summed + recv3[t]
-    live = lax.broadcasted_iota(jnp.int32, summed.shape, 0) < shard_rows
-    summed = jnp.where(live, summed, 0.0)
-
-    squares = summed * summed
-    norm_line[spot] = squares[0:8] + squares[8:16] + squares[16:24] + squares[24:32]
+        tails[plane + 1] += tails[plane]
+
+    norm_line[spot] = tails[plane + 1]
     gsum[z] = summed
 
     def line_copy(t):
@@ -488,9 +510,11 @@
     loop(1, line, lambda t: line_copy(t).start())
     loop(1, depth, lambda t: spread_sum(t).start())
     loop(1, line, lambda t: line_got(t).wait_recv())
-    sumsq = norm_line[0]
+    line_sums = norm_line[0]
     for n in range(1, line):
-        sumsq = sumsq + norm_line[n]
+        line_sums = line_sums + norm_line[n]
+    entries_sum = jnp.where(spare, 0.0, line_sums)
+    sumsq = jnp.where(spare, line_sums, entries_sum * entries_sum)
     norm_plane[p] = sumsq
 
     def plane_copy(t):
@@ -504,6 +528,12 @@
     loop(1, plane, lambda t: plane_copy(t).start())
     loop(1, depth, lambda t: state_got(t).wait_recv())
     loop(1, depth, lambda t: sum_got(t).wait_recv())
+    loop(1, depth, lambda t: spread_sum(t).wait_send())
+
+    @pl.when(owns_tail)
+    def _():
+        gsum[tail_z, pl.ds(tail_row, 8)] += entries_sum
+
     loop(1, plane, lambda t: plane_got(t).wait_recv())
     sumsq = norm_plane[0]
     for n in range(1, plane):
@@ -656,12 +686,13 @@
     tail_ref[...] = flat[used : used + 8, :]
 
     loop(0, plane, lambda t: pair(t).wait_send())
-    loop(0, own_t, lambda t: across(t).wait_send())
+    loop(far, own_t, lambda t: across(t).wait_send())
     loop(1, depth, lambda t: along(t).wait_send())
     loop(1, line, lambda t: line_copy(t).wait_send())
     loop(1, plane, lambda t: plane_copy(t).wait_send())
     loop(1, depth, lambda t: spread_state(t).wait_send())
-    loop(1, depth, lambda t: spread_sum(t).wait_send())
+    loop(1, depth, lambda t: far_along(t).wait_send())
+    loop(0, far, lambda t: far_across(t).wait_send())
 
     @pl.when(core != tail_core)
     def _():
@@ -670,10 +701,6 @@
     @pl.when(jnp.logical_and(owns_tail, p != tail_place))
     def _():
         tail_across(tail_t).wait_send()
-
-    @pl.when(jnp.logical_and(at_tail, z != tail_z))
-    def _():
-        tail_along(tail_zt).wait_send()
 
     def all_sent(n):
         a, b = n // w_size, n % w_size
@@ -698,6 +725,7 @@
     flat_rows = plane * line * master.shape[0] + PAD_ROWS
     shard = pltpu.VMEM(master.shape, f32)
     weight = weight.reshape(9, channels, channels)
+    far = 4
     ring_w = 2 * split_rows
     ring_x = plane // ring_w
     gathered = (2, ring_x, ring_w, depth, PAD_ROWS, LANES)
@@ -727,13 +755,13 @@
             pltpu.VMEM(gathered, bf16),
             pltpu.VMEM((3, channels, LANES), f32),
             pltpu.VMEM((3 * channels, height * width), bf16),
-            pltpu.VMEM((wide, height * width), bf16),
+            pltpu.VMEM((wide, (height + 2) * width), bf16),
             pltpu.VMEM((3 * channels, wide), bf16),
             pltpu.VMEM((wide // LANES, 3 * channels, LANES), f32),
             pltpu.VMEM((flat_rows, LANES), f32),
             pltpu.VMEM((height, channels, width), f32),
             pltpu.VMEM((height, channels, width), f32),
-            pltpu.VMEM((height + 2, channels, width), f32),
+            pltpu.VMEM((height, channels, width), f32),
             pltpu.VMEM(part, bf16),
             pltpu.VMEM(part, bf16),
             pltpu.VMEM(part, bf16),
@@ -745,13 +773,16 @@
             pltpu.VMEM((line, 8, LANES), f32),
             pltpu.VMEM((plane, 8, LANES), f32),
             pltpu.VMEM((plane + 2, 8, LANES), f32),
-            pltpu.VMEM((depth, 8, LANES), f32),
+            pltpu.VMEM((depth, far, PAD_ROWS, LANES), bf16),
+            pltpu.VMEM((depth, far, PAD_ROWS, LANES), bf16),
+            pltpu.VMEM((far, PAD_ROWS, LANES), f32),
+            pltpu.VMEM((far, PAD_ROWS, LANES), f32),
             dma(8),
         ]
         + [dma(n) for n in (plane, plane, plane, plane, depth, depth, line, line)]
         + [dma(n) for n in (plane, plane, depth, depth, depth, depth)]
         + [dma(2, ring_x, ring_w)] * 4
-        + [dma(3), dma(plane + depth)],
+        + [dma(2), dma(plane), dma(depth), dma(depth), dma(far), dma(far)],
         compiler_params=pltpu.CompilerParams(
             collective_id=0, has_side_effects=True, vmem_limit_bytes=VMEM_LIMIT
         ),

time: 68.7 us -> 65.1 us (0.948)
  Pallas kernels: 68 us -> 64.4 us
    pallas_call x1, Pallas kernels: 65.6 us -> 62 us  [run_layer(): pl.pallas_call(functools.partial(layer_kernel, split_rows, plane, depth),...]
where the time goes in v6:
time: 65.1 us; the launch traced here: 65 us
  Pallas kernels  64.4 us (99%)
    pallas_call x1, Pallas kernels, run_layer(): pl.pallas_call(functools.partial(layer_kernel, split_rows, plane, depth),...  62 us
    pallas_call x1, Pallas kernels, finish(): pl.pallas_call(finish_kernel, out_shape=tuple((jax.ShapeDtypeStruct(r.sha...  2.41 us

profile of v6, /device:TPU:1, one launch (start us, length us, event | category | flops | bytes accessed | tf_op | source)
XLA Modules:
  0.0 65.0 jit_solution(119237725407326032)
XLA Ops:
  0.6 62.0 %shard_map.143 = (bf16[16,320,128]{2,1,0:T(8,128)(2,1)S(1)}, bf16[2880,320]{1,0:T(8,128)(2,1)S(1)}, f32[8,128]{1,0:T(8,128)S(1)}, f32[29,128]{1,0:T(8,128)S(1)},...) custom-call(bf16[16,320,128]{2,1,0:T(8,128)(2,1)} %bitcast.18, bf16[16,320,128]{2,1,0:T(8,128)(2,1)} %bitcast.19, ...), custom_call_target="tpu_custom_call" | custom-call | tf_op jit(solution)/shard_map/pallas_call | solution.py:737
  62.6 2.4 %shard_map.144 = (bf16[16,320,128]{2,1,0:T(8,128)(2,1)}, bf16[2880,320]{1,0:T(8,128)(2,1)}, f32[29,128]{1,0:T(8,128)}, f32[29,128]{1,0:T(8,128)}, f32[29,128]{1,...) custom-call(f32[8,128]{1,0:T(8,128)S(1)} %get-tuple-element.22.tail_ref, ...), custom_call_target="tpu_custom_call" | custom-call | tf_op jit(solution)/shard_map/pallas_call | solution.py:817

commit v7 on v6

--- a/solution.py
+++ b/solution.py
@@ -71,6 +71,7 @@
     send2,
     recv2,
     acc,
+    accb,
     recv3,
     state,
     gsum,
@@ -449,8 +450,9 @@
     loop(far, own_t, across_take)
 
     def along(t):
-        return copy(acc.at[(z + t) % depth], recv3.at[t], s3.at[t], r3.at[t], in_depth(t))
-
+        return copy(accb.at[(z + t) % depth], recv3.at[t], s3.at[t], r3.at[t], in_depth(t))
+
+    accb[...] = acc[...].astype(bf16)
     loop(1, depth, lambda t: along(t).start())
     def input_step(r, carry):
         slope = gact[r] * gain
@@ -462,7 +464,7 @@
     loop(1, depth, lambda t: along(t).wait_recv())
     summed = acc[z]
     for t in range(1, depth):
-        summed = summed + recv3[t]
+        summed = summed + recv3[t].astype(f32)
     loop(0, far, lambda t: far_across(t).wait_recv())
     for t in range(far):
         summed = summed + recvf[t]
@@ -767,7 +769,8 @@
             pltpu.VMEM(part, bf16),
             pltpu.VMEM(part, bf16),
             pltpu.VMEM((depth, PAD_ROWS, LANES), f32),
-            pltpu.VMEM((depth, PAD_ROWS, LANES), f32),
+            pltpu.VMEM((depth, PAD_ROWS, LANES), bf16),
+            pltpu.VMEM((depth, PAD_ROWS, LANES), bf16),
             pltpu.VMEM((depth, 3, PAD_ROWS, LANES), f32),
             pltpu.VMEM((depth, PAD_ROWS, LANES), f32),
             pltpu.VMEM((line, 8, LANES), f32),

time: 65.1 us -> 64.7 us (level)
  no operation moved by 1% of the time
where the time goes in v7:
time: 64.7 us; the launch traced here: 64.6 us
  Pallas kernels  64 us (99%)
    pallas_call x1, Pallas kernels, run_layer(): pl.pallas_call(functools.partial(layer_kernel, split_rows, plane, depth),...  61.6 us
    pallas_call x1, Pallas kernels, finish(): pl.pallas_call(finish_kernel, out_shape=tuple((jax.ShapeDtypeStruct(r.sha...  2.41 us

profile of v7, /device:TPU:1, one launch (start us, length us, event | category | flops | bytes accessed | tf_op | source)
XLA Modules:
  0.0 64.6 jit_solution(12437872130257416600)
XLA Ops:
  0.6 61.6 %shard_map.143 = (bf16[16,320,128]{2,1,0:T(8,128)(2,1)S(1)}, bf16[2880,320]{1,0:T(8,128)(2,1)S(1)}, f32[8,128]{1,0:T(8,128)S(1)}, f32[29,128]{1,0:T(8,128)S(1)},...) custom-call(bf16[16,320,128]{2,1,0:T(8,128)(2,1)} %bitcast.18, bf16[16,320,128]{2,1,0:T(8,128)(2,1)} %bitcast.19, ...), custom_call_target="tpu_custom_call" | custom-call | tf_op jit(solution)/shard_map/pallas_call | solution.py:739
  62.2 2.4 %shard_map.144 = (bf16[16,320,128]{2,1,0:T(8,128)(2,1)}, bf16[2880,320]{1,0:T(8,128)(2,1)}, f32[29,128]{1,0:T(8,128)}, f32[29,128]{1,0:T(8,128)}, f32[29,128]{1,...) custom-call(f32[8,128]{1,0:T(8,128)S(1)} %get-tuple-element.22.tail_ref, ...), custom_call_target="tpu_custom_call" | custom-call | tf_op jit(solution)/shard_map/pallas_call | solution.py:820
